TPU v7x, 256 devices: a whole 4x4x8 slice. The times are simulated.
256 devices in a mesh: aux: 16 (over x_hi, z), row: 16 (over y, x_lo, core).
Axes of the slice: x: 4 (x_hi: 2, x_lo: 2; x = x_hi * 2 + x_lo), y: 4, z: 8, core: 2. Of those that a mesh axis runs over, the one named last changes fastest.
Arguments:
- factors: float32 [48, 3072, 3072], P('aux', 'row'), may hold values from -0.109375 to 0.109375
- orbitals: float32 [3072, 512], P('row'), may hold values from -1.25 to 1.25
- tile_mask: int32 [48, 24, 24], P('aux'), may hold values from 0 to 1, as said below
Outputs:
- exchange: float32 [3072, 3072], P('aux', 'row')
Inputs may be any that keep to these rules, and one draw needn't show every extreme that they name: `tile_mask`: each auxiliary function has its own share of surviving tiles, from about three tenths to all of them.
All inputs are finite; a program needn't handle non-finite values.
Results may differ from a plain program's by a relative error of at most 0.0001.
Values sent between devices are 32-bit elements; how exact they have to be, the bound alone decides.
A program may use at most 128 MiB of HBM per device.

v0:
```python
import jax
import jax.numpy as jnp
from jax import lax
from jax.sharding import PartitionSpec as P


def per_device(factors, orbitals, tile_mask):
    slabs, rows_local, nbf = factors.shape
    tiles = tile_mask.shape[1]
    tile_width = nbf // tiles
    row_start = lax.axis_index("row") * rows_local
    tile_of_row = (row_start + jnp.arange(rows_local, dtype=jnp.int32)) // tile_width
    onehot = (tile_of_row[:, None] == jnp.arange(tiles, dtype=jnp.int32)[None, :]).astype(
        jnp.float32
    )
    mask_rows = jnp.einsum("rt,stu->sru", onehot, tile_mask.astype(jnp.float32))
    screened = factors * jnp.repeat(mask_rows, tile_width, axis=2)
    half = jnp.einsum(
        "src,ci->sri",
        screened,
        lax.all_gather(orbitals, "row", axis=0, tiled=True),
        precision=lax.Precision.HIGHEST,
        preferred_element_type=jnp.float32,
    )
    all_rows = lax.all_gather(half, "row", axis=1, tiled=True)
    return lax.psum_scatter(
        jnp.einsum(
            "sci,sri->cr",
            all_rows,
            half,
            precision=lax.Precision.HIGHEST,
            preferred_element_type=jnp.float32,
        ),
        "aux",
        scatter_dimension=0,
        tiled=True,
    )


def solution(mesh):
    placed = (P("aux", "row", None), P("row", None), P("aux", None, None))
    return jax.shard_map(
        per_device, mesh=mesh, in_specs=placed, out_specs=P("aux", "row"), check_vma=False
    )
```

profile of v0, /device:TPU:39, one launch (start us, length us, event | category | flops | bytes accessed | tf_op | source)
XLA Modules:
  0.0 408.7 jit_solution(3004344993074710556)
XLA Ops:
  6.5 0.0 all-gather.3.cloned.1.call-start
  6.5 0.7 all-gather.3.cloned.1.call-update
  7.3 0.0 all-gather.5.cloned.1.call-start
  7.3 0.8 convert_element_type.4
  8.1 0.1 copy.4
  8.2 0.1 fusion.3
  8.3 0.2 copy.5
  8.5 4.1 %broadcast_in_dim.2 = f32[3,192,24,128]{3,2,1,0:T(8,128)} broadcast(f32[3,192,24]{2,1,0:T(8,128)S(1)} %copy.5), dimensions={0,1,2} | broadcast | bytes 7133184 | tf_op jit(solution)/shard_map/broadcast_in_dim | solution.py:17
  12.6 8.4 %reshape.22 = f32[3,192,3072]{2,1,0:T(8,128)} reshape(f32[3,192,24,128]{3,2,1,0:T(8,128)} %broadcast_in_dim.2) | data formatting | bytes 14155776 | tf_op jit(solution)/shard_map/reshape | solution.py:17
  20.9 36.0 %all-gather.3.cloned.1.call-done = f32[3072,512]{1,0:T(8,128)} async-done(((f32[192,512]{1,0:T(8,128)}), f32[3072,512]{1,0:T(8,128)}) %all-gather.3.cloned.1.call-update) | async-done | bytes 6291472 | tf_op jit(solution)/shard_map/all_gather | solution.py:21
  56.9 15.9 %fusion = f32[3,192,512]{2,1,0:T(8,128)} fusion(f32[3,192,3072]{2,1,0:T(8,128)} %param.3, f32[3,192,3072]{2,1,0:T(8,128)} %reshape.22, f32[3072,512]{1,0:T(8,128)} %all-gather.3.cloned.1.call-done), kind=kOutput, calls=%fused_computation | convolution fusion | flops 10873405440 | bytes 21626880 | tf_op jit(solution)/shard_map/src,ci->sri/dot_general | solution.py:18
  72.8 0.0 all-gather.5.cloned.1.call-update
  72.9 0.0 reduce-scatter.2.cloned.1.call-start
  72.9 105.0 %all-gather.5.cloned.1.call-done = f32[3,3072,512]{2,1,0:T(8,128)} async-done(((f32[3,192,512]{2,1,0:T(8,128)}), f32[3,3072,512]{2,1,0:T(8,128)}) %all-gather.5.cloned.1.call-update) | async-done | bytes 18874384 | tf_op jit(solution)/shard_map/all_gather | solution.py:25
  177.9 19.3 %convolution_bitcast_fusion = f32[3072,192]{1,0:T(8,128)} fusion(f32[3,3072,512]{2,1,0:T(8,128)} %all-gather.5.cloned.1.call-done, f32[3,192,512]{2,1,0:T(8,128)} %fusion), kind=kOutput, calls=%fused_computation.3 | convolution fusion | flops 10871635968 | bytes 22413312 | tf_op jit(solution)/shard_map/sci,sri->cr/dot_general | solution.py:27
  197.2 0.0 reduce-scatter.2.cloned.1.call-update
  197.2 204.9 %reduce-scatter.2.cloned.1.call-done = f32[192,192]{1,0:T(8,128)} async-done(((f32[3072,192]{1,0:T(8,128)}), f32[192,192]{1,0:T(8,128)}) %reduce-scatter.2.cloned.1.call-update) | async-done | bytes 147472 | tf_op jit(solution)/shard_map/reduce_scatter | solution.py:26
  (1 shorter events, 0.0 us)
Async XLA Ops:
  6.5 50.4 %all-gather.3.cloned.1.call-start = ((), (), s32[]{:S(2)}) async-start(), calls=%async_computation.1 | async-start | bytes 6684672 | tf_op jit(solution)/shard_map/all_gather | solution.py:21
  7.3 170.7 %all-gather.5.cloned.1.call-start = ((), (), s32[]{:S(2)}) async-start(), calls=%async_computation.2 | async-start | bytes 20054016 | tf_op jit(solution)/shard_map/all_gather | solution.py:25
  72.9 329.3 %reduce-scatter.2.cloned.1.call-start = ((), (), s32[]{:S(2)}) async-start(), calls=%async_computation.3 | async-start | bytes 3342336 | tf_op jit(solution)/shard_map/reduce_scatter | solution.py:26
Sparse Core Ops, SparseCore 0:
  9.2 47.6 all-gather.2
  73.0 104.8 all-gather.4
  197.3 204.7 reduce-scatter.1
where the time goes:
time: 415 us; the launch traced here: 409 us
  waiting for transfers between devices  347 us (84%)
  matrix products  35.3 us (9%)
  between operations  13.1 us (3%)
  local copies, waits for them, and re-layouts  12.7 us (3%)
    reduce_scatter x1, waiting for transfers between devices, per_device(): lax.psum_scatter(jnp.einsum('sci,sri->cr', all_rows, half, precision=lax....  205 us
    all_gather x1, waiting for transfers between devices, per_device(): all_rows = lax.all_gather(half, 'row', axis=1, tiled=True)  105 us
    all_gather x1, waiting for transfers between devices, per_device(): lax.all_gather(orbitals, 'row', axis=0, tiled=True)  36 us
    dot_general x1, matrix products, per_device(): jnp.einsum('sci,sri->cr', all_rows, half, precision=lax.Precision.HIGHEST...  19.3 us
    dot_general x1, matrix products, per_device(): jnp.einsum('src,ci->sri', screened, lax.all_gather(orbitals, 'row', axis=...  15.9 us
    reshape x1, local copies, waits for them, and re-layouts, per_device(): screened = factors * jnp.repeat(mask_rows, tile_width, axis=2)  8.35 us
  transfers between devices with their start and end apart: 3, of which 3 were waited for; matrix products, arithmetic and copies ran while one was open for 3% of the time, Pallas kernels for 0%

commit v1 on v0

v1 whole, which is shorter than its diff:
```python
import jax
import jax.numpy as jnp
from jax import lax
from jax.experimental import pallas as pl
from jax.experimental.pallas import tpu as pltpu
from jax.sharding import PartitionSpec as P

F32 = jnp.float32
BF16 = jnp.bfloat16
MESH = pl.DeviceIdType.MESH
ROWS = 192
PAIR = 384
LANES = 128
CHUNKS = 4
SLABS = 3
STRIP = 24
STEPS_Y = (1, -1, 2)


def split(value):
    high = value.astype(BF16)
    return high, (value - high.astype(F32)).astype(BF16)


def kernel(
    b_hbm, c_ref, mask, out,
    bf, bh, bl, cb, ch, hs, ho, hy, hx, hw, left, right, kp, rc, rp, rm, fp, rd, rt,
    sem_b, y_send, y_recv, x_send, x_recv, s_send, s_recv,
    h_send, ho_recv, hy_recv, hx_recv, hw_recv,
    core_send, core_recv, p_send, p_recv, m_send, m_recv, f_send, f_recv,
):
    a, r = lax.axis_index("aux"), lax.axis_index("row")
    xh, z = a // 8, a % 8
    y, xl, c = r // 4, (r // 2) % 2, r % 2
    sib = 1 - c

    def row_of(yy, xx, cc):
        return ((yy + 4) % 4 * 2 + xx) * 2 + cc

    def dev(yy, xx, cc):
        return (a, row_of(yy, xx, cc))

    def copy(src, dst, send, recv, to):
        return pltpu.make_async_remote_copy(
            src_ref=src, dst_ref=dst, send_sem=send, recv_sem=recv, device_id=to, device_id_type=MESH
        )

    across = ((a, row_of(y, 1 - xl, c)), ((1 - xh) * 8 + z, row_of(y, 1 - xl, c)))
    sibling = dev(y, xl, sib)
    z_up = (xh * 8 + (z + 1) % 8, r)
    z_down = (xh * 8 + (z + 7) % 8, r)

    slab_copies = [pltpu.make_async_copy(b_hbm.at[p], bf.at[p], sem_b.at[p]) for p in range(SLABS)]
    for each in slab_copies:
        each.start()

    barrier = pltpu.get_barrier_semaphore()
    greeted = [
        dev(y + 1, xl, c), dev(y - 1, xl, c), dev(y + 2, xl, c), across[0], across[1], sibling,
        dev(y + 1, xl, sib), dev(y, 1 - xl, sib), dev(y + 2, xl, sib), z_up, z_down,
    ]
    for each in greeted:
        pl.semaphore_signal(barrier, inc=1, device_id=each, device_id_type=MESH)
    for k in range(CHUNKS):
        cb[k, r] = c_ref[:, k * LANES : (k + 1) * LANES]
    pl.semaphore_wait(barrier, len(greeted))

    def to_y(k, j):
        return copy(cb.at[k, r], cb.at[k, r], y_send.at[k, j], y_recv.at[k, j], dev(y + STEPS_Y[j], xl, c))

    def from_y(k, j):
        block = row_of(y - STEPS_Y[j], xl, c)
        return copy(cb.at[k, block], cb.at[k, block], y_send.at[k, j], y_recv.at[k, j], sibling)

    def to_x(k, j, block, part):
        piece = cb.at[k, block, pl.ds(96 * part, 96)]
        return copy(piece, piece, x_send.at[k, j, part], x_recv.at[k, j, part], across[part])

    def to_sibling(k, j, block):
        return copy(cb.at[k, block], cb.at[k, block], s_send.at[k, j], s_recv.at[k, j], sibling)

    def y_block(j, xx, cc):
        return row_of(y - STEPS_Y[j], xx, cc) if j < 3 else row_of(y, xx, cc)

    def first(k):
        for j in range(3):
            to_y(k, j).start()
        for part in range(2):
            to_x(k, 3, r, part).start()
        to_sibling(k, 3, r).start()

    def forward_y(k):
        for j in range(3):
            from_y(k, j).wait_recv()
            block = y_block(j, xl, c)
            for part in range(2):
                to_x(k, j, block, part).start()
            to_sibling(k, j, block).start()

    def forward_x(k):
        for j in (3, 0, 1, 2):
            block = y_block(j, 1 - xl, c)
            for part in range(2):
                to_x(k, j, block, part).wait_recv()
            to_sibling(k, 4 + j, block).start()

    def whole(k):
        for j in range(4):
            to_sibling(k, j, y_block(j, xl, sib)).wait_recv()
            to_sibling(k, 4 + j, y_block(j, 1 - xl, sib)).wait_recv()

    def screen(p):
        slab_copies[p].wait()

        def tile(n, _):
            at = pl.ds(pl.multiple_of(n * LANES, LANES), LANES)
            for g in range(3):
                keep = mask[p, (3 * r + g) // 2, n].astype(F32)
                rows = pl.ds(64 * g, 64)
                high, low = split(bf[p, rows, at] * keep)
                bh[p, rows, at] = high
                bl[p, rows, at] = low
            return 0

        lax.fori_loop(0, 24, tile, 0, unroll=4)

    def half(k):
        def block(n, _):
            high, low = split(cb[k, n])
            at = pl.ds(pl.multiple_of(n * ROWS, ROWS), ROWS)
            ch[at, 0:LANES] = high
            ch[at, LANES : 2 * LANES] = low
            return 0

        lax.fori_loop(0, 16, block, 0)

        def slab(p, _):
            both = jnp.dot(bh[p], ch[...], preferred_element_type=F32)
            low = jnp.dot(bl[p], ch[:, 0:LANES], preferred_element_type=F32)
            hs[k, p] = both[:, 0:LANES] + (both[:, LANES : 2 * LANES] + low)
            return 0

        lax.fori_loop(0, SLABS, slab, 0)

    def h_copies(k):
        h, q = k % 2, k // 2
        return (
            copy(hs.at[k], hy.at[q, c], h_send.at[k, 0], hy_recv.at[q, c], dev(y - 1, xl, h)),
            copy(hs.at[k], hx.at[q, c], h_send.at[k, 1], hx_recv.at[q, c], dev(y, 1 - xl, h)),
            copy(hs.at[k], hw.at[c], h_send.at[k, 2], hw_recv.at[c], dev(y + 2, xl, h)),
            copy(hs.at[k], ho.at[q], h_send.at[k, 3], ho_recv.at[q], sibling),
        )

    def send_half(k):
        to_1, to_2, to_3, to_4 = h_copies(k)
        to_1.start()
        to_2.start()
        pl.when(k // 2 == 1 - y // 2)(to_3.start)
        pl.when(k % 2 != c)(to_4.start)

    first(0)
    first(1)
    kp[...] = jnp.zeros_like(kp)
    screen(0)
    forward_y(0)
    first(2)
    screen(1)
    forward_y(1)
    first(3)
    forward_x(0)
    screen(2)

    def step(k, _):
        @pl.when(k < CHUNKS - 2)
        def _():
            forward_y(k + 2)

        @pl.when(k < CHUNKS - 1)
        def _():
            forward_x(k + 1)

        whole(k)
        half(k)
        send_half(k)
        return 0

    lax.fori_loop(0, CHUNKS, step, 0)

    def operand(slot, core, p, value):
        rows = pl.ds(pl.multiple_of(core * ROWS, ROWS), ROWS)
        high, low = split(value)
        for where, part in ((0, high), (1, low), (2, high)):
            left[slot, rows, pl.ds((where * SLABS + p) * LANES, LANES)] = part
        if slot in (0, 2):
            for where, part in ((0, high), (1, high), (2, low)):
                right[slot // 2, rows, pl.ds((where * SLABS + p) * LANES, LANES)] = part

    def product(kind, _):
        g, t = kind // 3, kind % 3
        value = lax.dot_general(
            left[2 * g + (t + 1) // 2], right[t // 2], (((1,), (1,)), ((), ())), preferred_element_type=F32
        )
        kp[kind] = kp[kind] + value.reshape(8, 2, STRIP, PAIR)
        return 0

    def core_copy(g):
        kinds = pl.ds(3 * g, 3)
        return copy(kp.at[kinds, :, sib], rc.at[kinds], core_send.at[g], core_recv.at[g], sibling)

    def core_arrival(g):
        kinds = pl.ds(3 * g, 3)
        return copy(rc.at[kinds], rc.at[kinds], core_send.at[g], core_recv.at[g], sibling)

    def products(q, _):
        k = 2 * q + c
        copy(ho.at[q], ho.at[q], h_send.at[k, 3], ho_recv.at[q], sibling).wait_recv()
        for core in range(2):
            copy(hy.at[q, core], hy.at[q, core], h_send.at[k, 0], hy_recv.at[q, core], sibling).wait_recv()
            copy(hx.at[q, core], hx.at[q, core], h_send.at[k, 1], hx_recv.at[q, core], sibling).wait_recv()
        for p in range(SLABS):
            operand(0, c, p, hs[k, p])
            operand(0, sib, p, ho[q, p])
            for core in range(2):
                operand(1, core, p, hy[q, core, p])
                operand(2, core, p, hx[q, core, p])
        lax.fori_loop(0, 3, product, 0)

        @pl.when(q == 1)
        def _():
            core_copy(0).start()

        @pl.when(q == xl)
        def _():
            lax.fori_loop(3, 4, product, 0)

        @pl.when(q == y // 2)
        def _():
            for core in range(2):
                copy(hw.at[core], hw.at[core], h_send.at[k, 2], hw_recv.at[core], sibling).wait_recv()
            for p in range(SLABS):
                for core in range(2):
                    operand(3, core, p, hw[core, p])
            lax.fori_loop(4, 6, product, 0)

        return 0

    lax.fori_loop(0, 2, products, 0)
    core_copy(1).start()

    def up_copy(s, g):
        kinds = pl.ds(3 * g, 3)
        return copy(rc.at[kinds, (z + 4 - s) % 8], rp.at[s, kinds], p_send.at[s, g], p_recv.at[s, g], z_up)

    def down_copy(s, g):
        kinds = pl.ds(3 * g, 3)
        return copy(rc.at[kinds, (z + 5 + s) % 8], rm.at[s, kinds], m_send.at[s, g], m_recv.at[s, g], z_down)

    for s in range(5):
        for g in range(2):
            kinds = slice(3 * g, 3 * g + 3)
            if s == 0:
                core_arrival(g).wait_recv()

                def add(d, _, kinds=kinds):
                    rc[kinds, d] = rc[kinds, d] + kp[kinds, d, c]
                    return 0

                lax.fori_loop(0, 8, add, 0)
            else:
                up_copy(s - 1, g).wait_recv()
                d = (z + 4 - s) % 8
                rc[kinds, d] = rc[kinds, d] + rp[s - 1, kinds]
                if s < 4:
                    down_copy(s - 1, g).wait_recv()
                    d = (z + 5 + s) % 8
                    rc[kinds, d] = rc[kinds, d] + rm[s - 1, kinds]
            if s < 4:
                up_copy(s, g).start()
            if s < 3:
                down_copy(s, g).start()

    def strip_copies(kind, cj):
        g, t = kind // 3, kind % 3
        slot = 2 * g + (t + 1) // 2
        i_y = y + (slot % 2) * (1 + slot // 2)
        i_x = jnp.where(slot == 2, 1 - xl, xl)
        j_x = jnp.where(t == 2, 1 - xl, xl)
        at_i = row_of(i_y, i_x, z // 4)
        at_j = row_of(y, j_x, cj)
        where = (xh, 2 * (z % 4) + c)
        src = fp.at[kind, cj]
        straight = ((at_i, at_j), rd.at[where], f_recv.at[0])
        turned = ((at_j, at_i), rt.at[where], f_recv.at[1])
        return src, straight, turned

    def send_strips(n, _):
        kind, cj = n // 2, n % 2
        src, straight, turned = strip_copies(kind, cj)
        for which, (to, dst, recv) in enumerate((straight, turned)):
            here = jnp.logical_and(to[0] == a, to[1] == r)
            wanted = kind >= which

            @pl.when(jnp.logical_and(wanted, here))
            def _():
                pltpu.make_async_copy(src, dst, recv).start()

            @pl.when(jnp.logical_and(wanted, jnp.logical_not(here)))
            def _():
                copy(src, dst, f_send.at[kind, cj, which], recv, to).start()

        return 0

    def wait_strips(n, _):
        kind, cj = n // 2, n % 2
        src, straight, turned = strip_copies(kind, cj)
        for which, (to, dst, recv) in enumerate((straight, turned)):
            here = jnp.logical_and(to[0] == a, to[1] == r)

            @pl.when(jnp.logical_and(kind >= which, jnp.logical_not(here)))
            def _():
                copy(src, dst, f_send.at[kind, cj, which], recv, to).wait_send()

        return 0

    for kind in range(6):
        total = rc[kind, z]
        for cj in range(2):
            fp[kind, cj] = total[:, cj * ROWS : (cj + 1) * ROWS]
    lax.fori_loop(0, 12, send_strips, 0)

    def sent(k, _):
        for j in range(3):
            to_y(k, j).wait_send()
        for j in range(4):
            for part in range(2):
                to_x(k, j, r, part).wait_send()
        for j in range(8):
            to_sibling(k, j, r).wait_send()
        to_1, to_2, to_3, to_4 = h_copies(k)
        to_1.wait_send()
        to_2.wait_send()
        pl.when(k // 2 == 1 - y // 2)(to_3.wait_send)
        pl.when(k % 2 != c)(to_4.wait_send)
        return 0

    lax.fori_loop(0, CHUNKS, sent, 0)
    for g in range(2):
        core_copy(g).wait_send()
        for s in range(4):
            up_copy(s, g).wait_send()
        for s in range(3):
            down_copy(s, g).wait_send()

    apart = (y - a // 4 + 4) % 4
    across_x = xl != (a // 2) % 2

    @pl.when(apart != 1)
    def _():
        pltpu.make_async_copy(rd, rd, f_recv.at[0]).wait()
        out[...] = (rd[0] + rd[1]).reshape(ROWS, ROWS)

    @pl.when(apart == 1)
    def _():
        out[...] = jnp.zeros_like(out)

    @pl.when(jnp.logical_and(apart != 3, jnp.logical_or(apart != 0, across_x)))
    def _():
        pltpu.make_async_copy(rt, rt, f_recv.at[1]).wait()
        out[...] = out[...] + (rt[0] + rt[1]).reshape(ROWS, ROWS).T

    lax.fori_loop(0, 12, wait_strips, 0)


def per_device(factors, orbitals, tile_mask):
    dma = pltpu.SemaphoreType.DMA
    vmem = pltpu.VMEM
    part = (SLABS, ROWS, LANES)
    return pl.pallas_call(
        kernel,
        out_shape=jax.ShapeDtypeStruct((ROWS, ROWS), F32),
        in_specs=[
            pl.BlockSpec(memory_space=pl.ANY),
            pl.BlockSpec(memory_space=pltpu.VMEM),
            pl.BlockSpec(memory_space=pltpu.SMEM),
        ],
        out_specs=pl.BlockSpec(memory_space=pltpu.VMEM),
        scratch_shapes=[
            vmem((SLABS, ROWS, 3072), F32),
            vmem((SLABS, ROWS, 3072), BF16),
            vmem((SLABS, ROWS, 3072), BF16),
            vmem((CHUNKS, 16, ROWS, LANES), F32),
            vmem((3072, 2 * LANES), BF16),
            vmem((CHUNKS, *part), F32),
            vmem((2, *part), F32),
            vmem((2, 2, *part), F32),
            vmem((2, 2, *part), F32),
            vmem((2, *part), F32),
            vmem((4, PAIR, 3 * SLABS * LANES), BF16),
            vmem((2, PAIR, 3 * SLABS * LANES), BF16),
            vmem((6, 8, 2, STRIP, PAIR), F32),
            vmem((6, 8, STRIP, PAIR), F32),
            vmem((4, 6, STRIP, PAIR), F32),
            vmem((3, 6, STRIP, PAIR), F32),
            vmem((6, 2, STRIP, ROWS), F32),
            vmem((2, 8, STRIP, ROWS), F32),
            vmem((2, 8, STRIP, ROWS), F32),
            dma((SLABS,)),
            dma((CHUNKS, 3)), dma((CHUNKS, 3)),
            dma((CHUNKS, 4, 2)), dma((CHUNKS, 4, 2)),
            dma((CHUNKS, 8)), dma((CHUNKS, 8)),
            dma((CHUNKS, 4)), dma((2,)), dma((2, 2)), dma((2, 2)), dma((2,)),
            dma((2,)), dma((2,)),
            dma((4, 2)), dma((4, 2)), dma((3, 2)), dma((3, 2)),
            dma((6, 2, 2)), dma((2,)),
        ],
        compiler_params=pltpu.CompilerParams(
            collective_id=0, has_side_effects=True, vmem_limit_bytes=60 * 2**20
        ),
    )(factors, orbitals, tile_mask)


def solution(mesh):
    placed = (P("aux", "row", None), P("row", None), P("aux", None, None))
    return jax.shard_map(
        per_device, mesh=mesh, in_specs=placed, out_specs=P("aux", "row"), check_vma=False
    )
```

time: 415 us -> 128 us (0.31); the launches traced: 409 us -> 128 us
  waiting for transfers between devices: 347 us -> 0 us
  Pallas kernels: 0 us -> 126 us
  matrix products: 35.3 us -> 0 us
  between operations: 13.1 us -> 0.01 us
  local copies, waits for them, and re-layouts: 12.7 us -> 1.62 us
    reduce_scatter x1 -> x0, waiting for transfers between devices: 205 us -> none  [per_device(): lax.psum_scatter(jnp.einsum('sci,sri->cr', all_rows, half, precision=lax....]
    all_gather x2 -> x0, waiting for transfers between devices: 141 us -> none  [the longest x1 105 us: per_device(): all_rows = lax.all_gather(half, 'row', axis=1, tiled=True)]
    pallas_call x0 -> x1, Pallas kernels: none -> 126 us  [per_device(): pl.pallas_call(kernel, out_shape=jax.ShapeDtypeStruct((ROWS, ROWS), F32),...]
    dot_general x2 -> x0, matrix products: 35.2 us -> none  [the longest x1 19.3 us: per_device(): jnp.einsum('sci,sri->cr', all_rows, half, precision=lax.Precision.HIGHEST...]
    reshape x1 -> x0, local copies, waits for them, and re-layouts: 8.35 us -> none  [per_device(): screened = factors * jnp.repeat(mask_rows, tile_width, axis=2)]
  transfers between devices with their start and end apart: 3 -> 0, of which waited for: 3 -> 0; matrix products, arithmetic and copies ran while one was open for 3% -> 0% of each run, Pallas kernels for 0% -> 0%
where the time goes in v1:
time: 128 us
  Pallas kernels  126 us (98%)
  local copies, waits for them, and re-layouts  1.62 us (1%)
    pallas_call x1, Pallas kernels, per_device(): pl.pallas_call(kernel, out_shape=jax.ShapeDtypeStruct((ROWS, ROWS), F32),...  126 us

profile of v1, /device:TPU:39, one launch (start us, length us, event | category | flops | bytes accessed | tf_op | source)
XLA Modules:
  0.0 127.8 jit_solution(7904201119670634321)
XLA Ops:
  0.0 126.1 %shard_map.37 = f32[192,192]{1,0:T(8,128)} custom-call(f32[3,192,3072]{2,1,0:T(8,128)} %b_hbm.1, f32[192,512]{1,0:T(8,128)} %c_ref.1, s32[3,24,24]{2,1,0:T(8,128)} %mask.1), custom_call_target="tpu_custom_call" | custom-call | tf_op jit(solution)/shard_map/pallas_call | solution.py:378
  126.1 1.6 %copy.5 = f32[192,192]{1,0:T(8,128)} copy(f32[192,192]{1,0:T(8,128)} %shard_map.37) | data formatting | bytes 294912

commit v2 on v1

--- a/solution.py
+++ b/solution.py
@@ -13,7 +13,8 @@
 LANES = 128
 CHUNKS = 4
 SLABS = 3
-STRIP = 24
+STRIP = 48
+PACK = 72
 STEPS_Y = (1, -1, 2)
 
 
@@ -24,10 +25,10 @@
 
 def kernel(
     b_hbm, c_ref, mask, out,
-    bf, bh, bl, cb, ch, hs, ho, hy, hx, hw, left, right, kp, rc, rp, rm, fp, rd, rt,
+    bf, bh, bl, cb, ch, hs, ho, hy, hx, hw, left, right, kp, rc, rp, rm, re, fp, rd, rt, ft,
     sem_b, y_send, y_recv, x_send, x_recv, s_send, s_recv,
     h_send, ho_recv, hy_recv, hx_recv, hw_recv,
-    core_send, core_recv, p_send, p_recv, m_send, m_recv, f_send, f_recv,
+    core_send, core_recv, p_send, p_recv, m_send, m_recv, e_send, e_recv, f_send, f_recv,
 ):
     a, r = lax.axis_index("aux"), lax.axis_index("row")
     xh, z = a // 8, a % 8
@@ -197,15 +198,22 @@
 
     def product(kind, _):
         g, t = kind // 3, kind % 3
-        value = lax.dot_general(
-            left[2 * g + (t + 1) // 2], right[t // 2], (((1,), (1,)), ((), ())), preferred_element_type=F32
-        )
-        kp[kind] = kp[kind] + value.reshape(8, 2, STRIP, PAIR)
+        for core in range(2):
+            value = lax.dot_general(
+                left[2 * g + (t + 1) // 2],
+                right[t // 2, core * ROWS : (core + 1) * ROWS],
+                (((1,), (1,)), ((), ())),
+                preferred_element_type=F32,
+            )
+            rest = value[:, LANES:ROWS].reshape(8, 2, STRIP // 2, ROWS - LANES)
+            rest = jnp.concatenate([rest[:, 0], rest[:, 1]], axis=-1)
+            kp[core, kind, :, 0:STRIP] += value[:, 0:LANES].reshape(8, STRIP, LANES)
+            kp[core, kind, :, STRIP:PACK] += rest
         return 0
 
     def core_copy(g):
         kinds = pl.ds(3 * g, 3)
-        return copy(kp.at[kinds, :, sib], rc.at[kinds], core_send.at[g], core_recv.at[g], sibling)
+        return copy(kp.at[sib, kinds], rc.at[kinds], core_send.at[g], core_recv.at[g], sibling)
 
     def core_arrival(g):
         kinds = pl.ds(3 * g, 3)
@@ -247,22 +255,31 @@
     lax.fori_loop(0, 2, products, 0)
     core_copy(1).start()
 
+    mine = jnp.where(xh == y // 2, 0, 1)
+    groups = (1 - mine, mine)
+
+    def kinds_of(g):
+        return pl.ds(3 * g, 3)
+
     def up_copy(s, g):
-        kinds = pl.ds(3 * g, 3)
-        return copy(rc.at[kinds, (z + 4 - s) % 8], rp.at[s, kinds], p_send.at[s, g], p_recv.at[s, g], z_up)
+        src = rc.at[kinds_of(g), (z + 4 - s) % 8]
+        return copy(src, rp.at[s, kinds_of(g)], p_send.at[s, g], p_recv.at[s, g], z_up)
 
     def down_copy(s, g):
-        kinds = pl.ds(3 * g, 3)
-        return copy(rc.at[kinds, (z + 5 + s) % 8], rm.at[s, kinds], m_send.at[s, g], m_recv.at[s, g], z_down)
+        src = rc.at[kinds_of(g), (z + 5 + s) % 8]
+        return copy(src, rm.at[s, kinds_of(g)], m_send.at[s, g], m_recv.at[s, g], z_down)
+
+    def level_copy():
+        return copy(rc.at[kinds_of(1 - mine), z], re, e_send.at[0], e_recv.at[0], ((1 - xh) * 8 + z, r))
 
     for s in range(5):
-        for g in range(2):
-            kinds = slice(3 * g, 3 * g + 3)
+        for n, g in enumerate(groups):
+            kinds = kinds_of(g)
             if s == 0:
                 core_arrival(g).wait_recv()
 
                 def add(d, _, kinds=kinds):
-                    rc[kinds, d] = rc[kinds, d] + kp[kinds, d, c]
+                    rc[kinds, d] = rc[kinds, d] + kp[c, kinds, d]
                     return 0
 
                 lax.fori_loop(0, 8, add, 0)
@@ -278,24 +295,23 @@
                 up_copy(s, g).start()
             if s < 3:
                 down_copy(s, g).start()
-
-    def strip_copies(kind, cj):
-        g, t = kind // 3, kind % 3
-        slot = 2 * g + (t + 1) // 2
+            if s == 4 and n == 0:
+                level_copy().start()
+
+    def strip_copies(t):
+        kind = 3 * mine + t
+        slot = 2 * mine + (t + 1) // 2
         i_y = y + (slot % 2) * (1 + slot // 2)
         i_x = jnp.where(slot == 2, 1 - xl, xl)
         j_x = jnp.where(t == 2, 1 - xl, xl)
         at_i = row_of(i_y, i_x, z // 4)
-        at_j = row_of(y, j_x, cj)
-        where = (xh, 2 * (z % 4) + c)
-        src = fp.at[kind, cj]
-        straight = ((at_i, at_j), rd.at[where], f_recv.at[0])
-        turned = ((at_j, at_i), rt.at[where], f_recv.at[1])
-        return src, straight, turned
-
-    def send_strips(n, _):
-        kind, cj = n // 2, n % 2
-        src, straight, turned = strip_copies(kind, cj)
+        at_j = row_of(y, j_x, c)
+        straight = ((at_i, at_j), rd.at[z % 4], f_recv.at[0])
+        turned = ((at_j, at_i), rt.at[z % 4], f_recv.at[1])
+        return kind, fp.at[t], straight, turned
+
+    def send_strips(t, _):
+        kind, src, straight, turned = strip_copies(t)
         for which, (to, dst, recv) in enumerate((straight, turned)):
             here = jnp.logical_and(to[0] == a, to[1] == r)
             wanted = kind >= which
@@ -306,27 +322,24 @@
 
             @pl.when(jnp.logical_and(wanted, jnp.logical_not(here)))
             def _():
-                copy(src, dst, f_send.at[kind, cj, which], recv, to).start()
-
-        return 0
-
-    def wait_strips(n, _):
-        kind, cj = n // 2, n % 2
-        src, straight, turned = strip_copies(kind, cj)
+                copy(src, dst, f_send.at[t, which], recv, to).start()
+
+        return 0
+
+    def wait_strips(t, _):
+        kind, src, straight, turned = strip_copies(t)
         for which, (to, dst, recv) in enumerate((straight, turned)):
             here = jnp.logical_and(to[0] == a, to[1] == r)
 
             @pl.when(jnp.logical_and(kind >= which, jnp.logical_not(here)))
             def _():
-                copy(src, dst, f_send.at[kind, cj, which], recv, to).wait_send()
-
-        return 0
-
-    for kind in range(6):
-        total = rc[kind, z]
-        for cj in range(2):
-            fp[kind, cj] = total[:, cj * ROWS : (cj + 1) * ROWS]
-    lax.fori_loop(0, 12, send_strips, 0)
+                copy(src, dst, f_send.at[t, which], recv, to).wait_send()
+
+        return 0
+
+    level_copy().wait_recv()
+    fp[...] = rc[kinds_of(mine), z] + re[...]
+    lax.fori_loop(0, 3, send_strips, 0)
 
     def sent(k, _):
         for j in range(3):
@@ -351,13 +364,23 @@
         for s in range(3):
             down_copy(s, g).wait_send()
 
+    level_copy().wait_send()
+
     apart = (y - a // 4 + 4) % 4
     across_x = xl != (a // 2) % 2
+
+    def unpack(strips, block):
+        for n in range(4):
+            rest = strips[n, STRIP:PACK]
+            at = n * STRIP
+            block[at : at + STRIP, 0:LANES] = strips[n, 0:STRIP]
+            block[at : at + STRIP // 2, LANES:ROWS] = rest[:, 0 : ROWS - LANES]
+            block[at + STRIP // 2 : at + STRIP, LANES:ROWS] = rest[:, ROWS - LANES : LANES]
 
     @pl.when(apart != 1)
     def _():
         pltpu.make_async_copy(rd, rd, f_recv.at[0]).wait()
-        out[...] = (rd[0] + rd[1]).reshape(ROWS, ROWS)
+        unpack(rd, out)
 
     @pl.when(apart == 1)
     def _():
@@ -366,9 +389,10 @@
     @pl.when(jnp.logical_and(apart != 3, jnp.logical_or(apart != 0, across_x)))
     def _():
         pltpu.make_async_copy(rt, rt, f_recv.at[1]).wait()
-        out[...] = out[...] + (rt[0] + rt[1]).reshape(ROWS, ROWS).T
-
-    lax.fori_loop(0, 12, wait_strips, 0)
+        unpack(rt, ft)
+        out[...] = out[...] + ft[...].T
+
+    lax.fori_loop(0, 3, wait_strips, 0)
 
 
 def per_device(factors, orbitals, tile_mask):
@@ -397,13 +421,15 @@
             vmem((2, *part), F32),
             vmem((4, PAIR, 3 * SLABS * LANES), BF16),
             vmem((2, PAIR, 3 * SLABS * LANES), BF16),
-            vmem((6, 8, 2, STRIP, PAIR), F32),
-            vmem((6, 8, STRIP, PAIR), F32),
-            vmem((4, 6, STRIP, PAIR), F32),
-            vmem((3, 6, STRIP, PAIR), F32),
-            vmem((6, 2, STRIP, ROWS), F32),
-            vmem((2, 8, STRIP, ROWS), F32),
-            vmem((2, 8, STRIP, ROWS), F32),
+            vmem((2, 6, 8, PACK, LANES), F32),
+            vmem((6, 8, PACK, LANES), F32),
+            vmem((4, 6, PACK, LANES), F32),
+            vmem((3, 6, PACK, LANES), F32),
+            vmem((3, PACK, LANES), F32),
+            vmem((3, PACK, LANES), F32),
+            vmem((4, PACK, LANES), F32),
+            vmem((4, PACK, LANES), F32),
+            vmem((ROWS, ROWS), F32),
             dma((SLABS,)),
             dma((CHUNKS, 3)), dma((CHUNKS, 3)),
             dma((CHUNKS, 4, 2)), dma((CHUNKS, 4, 2)),
@@ -411,7 +437,8 @@
             dma((CHUNKS, 4)), dma((2,)), dma((2, 2)), dma((2, 2)), dma((2,)),
             dma((2,)), dma((2,)),
             dma((4, 2)), dma((4, 2)), dma((3, 2)), dma((3, 2)),
-            dma((6, 2, 2)), dma((2,)),
+            dma((1,)), dma((1,)),
+            dma((3, 2)), dma((2,)),
         ],
         compiler_params=pltpu.CompilerParams(
             collective_id=0, has_side_effects=True, vmem_limit_bytes=60 * 2**20

time: 128 us -> 116 us (0.906)
  Pallas kernels: 126 us -> 114 us
    pallas_call x1, Pallas kernels: 126 us -> 114 us  [per_device(): pl.pallas_call(kernel, out_shape=jax.ShapeDtypeStruct((ROWS, ROWS), F32),...]
where the time goes in v2:
time: 116 us
  Pallas kernels  114 us (98%)
  local copies, waits for them, and re-layouts  1.62 us (1%)
    pallas_call x1, Pallas kernels, per_device(): pl.pallas_call(kernel, out_shape=jax.ShapeDtypeStruct((ROWS, ROWS), F32),...  114 us

profile of v2, /device:TPU:39, one launch (start us, length us, event | category | flops | bytes accessed | tf_op | source)
XLA Modules:
  0.0 115.8 jit_solution(15947345746776437114)
XLA Ops:
  0.0 114.2 %shard_map.37 = f32[192,192]{1,0:T(8,128)} custom-call(f32[3,192,3072]{2,1,0:T(8,128)} %b_hbm.1, f32[192,512]{1,0:T(8,128)} %c_ref.1, s32[3,24,24]{2,1,0:T(8,128)} %mask.1), custom_call_target="tpu_custom_call" | custom-call | tf_op jit(solution)/shard_map/pallas_call | solution.py:402
  114.2 1.6 %copy.5 = f32[192,192]{1,0:T(8,128)} copy(f32[192,192]{1,0:T(8,128)} %shard_map.37) | data formatting | bytes 294912

commit v3 on v2

v3 whole, which is shorter than its diff:
```python
import jax
import jax.numpy as jnp
from jax import lax
from jax.experimental import pallas as pl
from jax.experimental.pallas import tpu as pltpu
from jax.sharding import PartitionSpec as P

F32 = jnp.float32
BF16 = jnp.bfloat16
MESH = pl.DeviceIdType.MESH
ROWS = 192
PAIR = 384
LANES = 128
CHUNKS = 4
PLANE = 2
SLICE = 24
SLABS = 3
STRIP = 48
PACK = 72
STEPS_Y = (1, -1, 2)


def split(value):
    high = value.astype(BF16)
    return high, (value - high.astype(F32)).astype(BF16)


def kernel(
    b_hbm, c_ref, mask, out,
    bf, bh, bl, cb, ch, hs, ho, hy, hx, hw, wr, left, right, kp, rc, rp, rm, re, fp, rd, rt, ft,
    sem_b, y_send, y_recv, x_send, x_recv, s_send, s_recv,
    g_send, g_recv, long_send, long_recv, short_send, short_recv, zs_send, zs_recv,
    h_send, ho_recv, hy_recv, hx_recv, hw_recv, wr_send, wr_recv,
    core_send, core_recv, p_send, p_recv, m_send, m_recv, e_send, e_recv, f_send, f_recv,
):
    a, r = lax.axis_index("aux"), lax.axis_index("row")
    xh, z = a // 8, a % 8
    y, xl, c = r // 4, (r // 2) % 2, r % 2
    sib = 1 - c

    def row_of(yy, xx, cc):
        return ((yy + 4) % 4 * 2 + xx) * 2 + cc

    def dev(yy, xx, cc):
        return (a, row_of(yy, xx, cc))

    def copy(src, dst, send, recv, to):
        return pltpu.make_async_remote_copy(
            src_ref=src, dst_ref=dst, send_sem=send, recv_sem=recv, device_id=to, device_id_type=MESH
        )

    across = ((a, row_of(y, 1 - xl, c)), ((1 - xh) * 8 + z, row_of(y, 1 - xl, c)))
    sibling = dev(y, xl, sib)
    z_up = (xh * 8 + (z + 1) % 8, r)
    z_down = (xh * 8 + (z + 7) % 8, r)

    slab_copies = [pltpu.make_async_copy(b_hbm.at[p], bf.at[p], sem_b.at[p]) for p in range(SLABS)]
    for each in slab_copies:
        each.start()

    here = 2 * y + xl
    for k in range(CHUNKS):
        cb[k, c, here] = c_ref[:, k * LANES : (k + 1) * LANES]

    barrier = pltpu.get_barrier_semaphore()
    peers = [dev(y + dy, xl, c) for dy in STEPS_Y] + [dev(y + dy, 1 - xl, c) for dy in (0, *STEPS_Y)]
    greeted = [
        *peers, across[1], sibling, z_up, z_down,
    ]
    for each in greeted:
        pl.semaphore_signal(barrier, inc=1, device_id=each, device_id_type=MESH)
    pl.semaphore_wait(barrier, len(greeted))

    def place(yy, xx):
        return (yy + 4) % 4 * 2 + xx

    def to_y(k, j):
        block = cb.at[k, c, here]
        return copy(block, block, y_send.at[k, j], y_recv.at[k, j], dev(y + STEPS_Y[j], xl, c))

    def from_y(k, j):
        block = cb.at[k, c, place(y - STEPS_Y[j], xl)]
        return copy(block, block, y_send.at[k, j], y_recv.at[k, j], sibling)

    def to_x(k, j, at, part):
        piece = cb.at[k, c, at, pl.ds(96 * part, 96)]
        return copy(piece, piece, x_send.at[k, j, part], x_recv.at[k, j, part], across[part])

    def to_sibling(k, j, at, core):
        block = cb.at[k, core, at]
        return copy(block, block, s_send.at[k, j], s_recv.at[k, j], sibling)

    def y_place(j, xx):
        return place(y - STEPS_Y[j], xx) if j < 3 else place(y, xx)

    def first(k):
        for j in range(3):
            to_y(k, j).start()
        for part in range(2):
            to_x(k, 3, here, part).start()
        to_sibling(k, 3, here, c).start()

    def forward_y(k):
        for j in range(3):
            from_y(k, j).wait_recv()
            at = y_place(j, xl)
            for part in range(2):
                to_x(k, j, at, part).start()
            to_sibling(k, j, at, c).start()

    def forward_x(k):
        for j in (3, 0, 1, 2):
            at = y_place(j, 1 - xl)
            for part in range(2):
                to_x(k, j, at, part).wait_recv()
            to_sibling(k, 4 + j, at, c).start()

    def slices(j, at):
        piece = cb.at[pl.ds(PLANE, CHUNKS - PLANE), c, at, pl.ds(SLICE * z, SLICE)]
        return copy(piece, piece, g_send.at[j], g_recv.at[j], peers[j])

    far = 1 - 2 * c
    z_far = (xh * 8 + (z + 8 + far) % 8, r)
    z_near = (xh * 8 + (z + 8 - far) % 8, r)

    def z_piece(k, core, at):
        return cb.at[k, core, :, pl.ds(SLICE * ((z + 8 + at) % 8), SLICE)]

    def to_far(k, s):
        piece = z_piece(k, c, -far * s)
        return copy(piece, piece, long_send.at[k, s], long_recv.at[k, s], z_far)

    def from_far(k, s):
        piece = z_piece(k, c, -far * (s + 1))
        return copy(piece, piece, long_send.at[k, s], long_recv.at[k, s], z_far)

    def to_near(k, s):
        piece = z_piece(k, c, far * s)
        return copy(piece, piece, short_send.at[k, s], short_recv.at[k, s], z_near)

    def from_near(k, s):
        piece = z_piece(k, c, far * (s + 1))
        return copy(piece, piece, short_send.at[k, s], short_recv.at[k, s], z_near)

    def z_sibling(k, core, j):
        piece = z_piece(k, core, j)
        at = (j + 8) % 8
        return copy(piece, piece, zs_send.at[k, at], zs_recv.at[k, at], sibling)

    def plane_slices():
        for j in range(7):
            slices(j, here).start()

    def z_first():
        for j in range(7):
            at = place(y - STEPS_Y[j], xl) if j < 3 else place(y, 1 - xl) if j == 3 else place(y - STEPS_Y[j - 4], 1 - xl)
            slices(j, at).wait_recv()

    def z_own(k):
        to_far(k, 0).start()
        to_near(k, 0).start()
        z_sibling(k, c, 0).start()

    def z_step(k, s):
        from_far(k, s).wait_recv()
        if s < 3:
            to_far(k, s + 1).start()
        z_sibling(k, c, -far * (s + 1)).start()
        if s < 3:
            from_near(k, s).wait_recv()
            if s < 2:
                to_near(k, s + 1).start()
            z_sibling(k, c, far * (s + 1)).start()

    def whole(k):
        if k < PLANE:
            for j in range(4):
                to_sibling(k, j, y_place(j, xl), sib).wait_recv()
                to_sibling(k, 4 + j, y_place(j, 1 - xl), sib).wait_recv()
        else:
            for j in range(8):
                z_sibling(k, sib, j).wait_recv()

    def screen(p):
        slab_copies[p].wait()

        def tile(n, _):
            at = pl.ds(pl.multiple_of(n * LANES, LANES), LANES)
            for g in range(3):
                keep = mask[p, (3 * r + g) // 2, n].astype(F32)
                rows = pl.ds(64 * g, 64)
                high, low = split(bf[p, rows, at] * keep)
                bh[p, rows, at] = high
                bl[p, rows, at] = low
            return 0

        lax.fori_loop(0, 24, tile, 0, unroll=4)

    def half(k):
        def block(n, _):
            high, low = split(cb[k, n % 2, n // 2])
            at = pl.ds(pl.multiple_of(n * ROWS, ROWS), ROWS)
            ch[at, 0:LANES] = high
            ch[at, LANES : 2 * LANES] = low
            return 0

        lax.fori_loop(0, 16, block, 0)

        def slab(p, _):
            both = jnp.dot(bh[p], ch[...], preferred_element_type=F32)
            low = jnp.dot(bl[p], ch[:, 0:LANES], preferred_element_type=F32)
            hs[k, p] = both[:, 0:LANES] + (both[:, LANES : 2 * LANES] + low)
            return 0

        lax.fori_loop(0, SLABS, slab, 0)

    def h_copies(k):
        h, q = k % 2, k // 2
        return (
            copy(hs.at[k], hy.at[q, c], h_send.at[k, 0], hy_recv.at[q, c], dev(y - 1, xl, h)),
            copy(hs.at[k], hx.at[q, c], h_send.at[k, 1], hx_recv.at[q, c], dev(y, 1 - xl, h)),
            copy(hs.at[k], wr.at[h], h_send.at[k, 2], wr_recv.at[h], dev(y + 1, xl, c)),
            copy(hs.at[k], ho.at[q], h_send.at[k, 3], ho_recv.at[q], sibling),
        )

    def send_half(k):
        to_1, to_2, to_3, to_4 = h_copies(k)
        to_1.start()
        to_2.start()
        pl.when(k // 2 == 1 - y // 2)(to_3.start)
        pl.when(k % 2 != c)(to_4.start)

    def relay_copy(k):
        h = k % 2
        return copy(wr.at[h], hw.at[c], wr_send.at[h], hw_recv.at[c], dev(y + 1, xl, h))

    def relays(k):
        return k // 2 == 1 - (y + 3) % 4 // 2

    def relay(k):
        @pl.when(relays(k))
        def _():
            h = k % 2
            copy(wr.at[h], wr.at[h], wr_send.at[h], wr_recv.at[h], sibling).wait_recv()
            relay_copy(k).start()

    plane_slices()
    first(0)
    kp[...] = jnp.zeros_like(kp)
    screen(0)
    z_first()
    z_own(2)
    forward_y(0)
    first(1)
    screen(1)
    z_step(2, 0)
    forward_x(0)
    forward_y(1)
    z_own(3)
    screen(2)
    z_step(2, 1)
    whole(0)
    half(0)
    send_half(0)
    forward_x(1)
    z_step(2, 2)
    z_step(3, 0)
    whole(1)
    half(1)
    send_half(1)
    z_step(2, 3)
    z_step(3, 1)
    whole(2)
    half(2)
    send_half(2)
    z_step(3, 2)
    z_step(3, 3)
    relay(0)
    relay(1)
    whole(3)
    half(3)
    send_half(3)
    relay(2)

    def operand(slot, core, p, value):
        rows = pl.ds(pl.multiple_of(core * ROWS, ROWS), ROWS)
        high, low = split(value)
        for where, part in ((0, high), (1, low), (2, high)):
            left[slot, rows, pl.ds((where * SLABS + p) * LANES, LANES)] = part
        if slot in (0, 2):
            for where, part in ((0, high), (1, high), (2, low)):
                right[slot // 2, rows, pl.ds((where * SLABS + p) * LANES, LANES)] = part

    def product(kind):
        rows, columns = ((0, 0), (1, 1), (1, 0), (2, 0), (3, 0), (3, 1))[kind]

        def one(core, _):
            at = pl.ds(pl.multiple_of(core * ROWS, ROWS), ROWS)
            value = lax.dot_general(
                left[rows], right[columns, at], (((1,), (1,)), ((), ())), preferred_element_type=F32
            )
            rest = value[:, LANES:ROWS].reshape(8, 2, STRIP // 2, ROWS - LANES)
            rest = jnp.concatenate([rest[:, 0], rest[:, 1]], axis=-1)
            kp[core, kind, :, 0:STRIP] += value[:, 0:LANES].reshape(8, STRIP, LANES)
            kp[core, kind, :, STRIP:PACK] += rest
            return 0

        lax.fori_loop(0, 2, one, 0)

    def kinds_of(g):
        start, count = ((0, 1), (1, 3), (4, 2))[g]
        return pl.ds(start, count)

    def core_copy(g):
        kinds = kinds_of(g)
        return copy(kp.at[sib, kinds], rc.at[kinds], core_send.at[g], core_recv.at[g], sibling)

    def core_arrival(g):
        kinds = kinds_of(g)
        return copy(rc.at[kinds], rc.at[kinds], core_send.at[g], core_recv.at[g], sibling)

    def take_o(q):
        copy(ho.at[q], ho.at[q], h_send.at[2 * q + c, 3], ho_recv.at[q], sibling).wait_recv()
        for p in range(SLABS):
            operand(0, c, p, hs[2 * q + c, p])
            operand(0, sib, p, ho[q, p])

    def take_y_x(q):
        k = 2 * q + c
        for core in range(2):
            copy(hy.at[q, core], hy.at[q, core], h_send.at[k, 0], hy_recv.at[q, core], sibling).wait_recv()
            copy(hx.at[q, core], hx.at[q, core], h_send.at[k, 1], hx_recv.at[q, core], sibling).wait_recv()
        for p in range(SLABS):
            for core in range(2):
                operand(1, core, p, hy[q, core, p])
                operand(2, core, p, hx[q, core, p])

    def products_y_x(q):
        product(1)
        product(2)
        pl.when(xl == q)(lambda: product(3))

    def products_w(q):
        @pl.when(y // 2 == q)
        def _():
            for core in range(2):
                copy(hw.at[core], hw.at[core], wr_send.at[core], hw_recv.at[core], sibling).wait_recv()
            for p in range(SLABS):
                for core in range(2):
                    operand(3, core, p, hw[core, p])
            product(4)
            product(5)

    mine = jnp.where(xh == y // 2, 0, 1)

    def up_copy(s, g):
        src = rc.at[kinds_of(g), (z + 4 - s) % 8]
        return copy(src, rp.at[s, kinds_of(g)], p_send.at[s, g], p_recv.at[s, g], z_up)

    def down_copy(s, g):
        src = rc.at[kinds_of(g), (z + 5 + s) % 8]
        return copy(src, rm.at[s, kinds_of(g)], m_send.at[s, g], m_recv.at[s, g], z_down)

    def sum_step(s, g):
        kinds = kinds_of(g)
        if s == 0:
            core_arrival(g).wait_recv()

            def add(d, _):
                rc[kinds, d] = rc[kinds, d] + kp[c, kinds, d]
                return 0

            lax.fori_loop(0, 8, add, 0)
        else:
            up_copy(s - 1, g).wait_recv()
            d = (z + 4 - s) % 8
            rc[kinds, d] = rc[kinds, d] + rp[s - 1, kinds]
            if s < 4:
                down_copy(s - 1, g).wait_recv()
                d = (z + 5 + s) % 8
                rc[kinds, d] = rc[kinds, d] + rm[s - 1, kinds]
        if s < 4:
            up_copy(s, g).start()
        if s < 3:
            down_copy(s, g).start()

    def level_copy(t):
        src = rc.at[2 * t + 1 - mine, z]
        return copy(src, re.at[t], e_send.at[t], e_recv.at[t], ((1 - xh) * 8 + z, r))

    def strip_copies(t):
        i_y = y + (mine, 1 - mine, 2)[t]
        i_x = (xl + mine) % 2 if t == 1 else xl
        j_x = xl if t == 1 else (xl + mine) % 2
        at_i = row_of(i_y, i_x, z // 4)
        at_j = row_of(y, j_x, c)
        straight = ((at_i, at_j), rd.at[z % 4], f_recv.at[0])
        turned = ((at_j, at_i), rt.at[z % 4], f_recv.at[1])
        return straight, turned

    def hand_out(t):
        level_copy(t).wait_recv()
        fp[t] = rc[2 * t + mine, z] + re[t]
        for which, (to, dst, recv) in enumerate(strip_copies(t)):
            own = jnp.logical_and(to[0] == a, to[1] == r)
            wanted = 2 * t + mine >= which

            @pl.when(jnp.logical_and(wanted, own))
            def _(dst=dst, recv=recv):
                pltpu.make_async_copy(fp.at[t], dst, recv).start()

            @pl.when(jnp.logical_and(wanted, jnp.logical_not(own)))
            def _(dst=dst, recv=recv, to=to, which=which):
                copy(fp.at[t], dst, f_send.at[t, which], recv, to).start()

    def handed_out(t):
        for which, (to, dst, recv) in enumerate(strip_copies(t)):
            own = jnp.logical_and(to[0] == a, to[1] == r)

            @pl.when(jnp.logical_and(2 * t + mine >= which, jnp.logical_not(own)))
            def _(dst=dst, recv=recv, to=to, which=which):
                copy(fp.at[t], dst, f_send.at[t, which], recv, to).wait_send()

    take_o(0)
    product(0)
    take_y_x(0)
    products_y_x(0)
    products_w(0)
    relay(3)
    take_o(1)
    product(0)
    core_copy(0).start()
    take_y_x(1)
    products_y_x(1)
    core_copy(1).start()
    sum_step(0, 0)
    sum_step(0, 1)
    sum_step(1, 0)
    sum_step(1, 1)
    products_w(1)
    core_copy(2).start()
    sum_step(2, 0)
    sum_step(2, 1)
    sum_step(0, 2)
    sum_step(3, 0)
    sum_step(3, 1)
    sum_step(1, 2)
    sum_step(4, 0)
    sum_step(4, 1)
    level_copy(0).start()
    level_copy(1).start()
    sum_step(2, 2)
    hand_out(0)
    hand_out(1)
    sum_step(3, 2)
    sum_step(4, 2)
    level_copy(2).start()
    hand_out(2)

    def sent(k, _):
        to_1, to_2, to_3, to_4 = h_copies(k)
        to_1.wait_send()
        to_2.wait_send()
        pl.when(k // 2 == 1 - y // 2)(to_3.wait_send)
        pl.when(k % 2 != c)(to_4.wait_send)
        pl.when(relays(k))(relay_copy(k).wait_send)
        return 0

    def sent_plane(k, _):
        for j in range(3):
            to_y(k, j).wait_send()
        for j in range(4):
            for part in range(2):
                to_x(k, j, here, part).wait_send()
        for j in range(8):
            to_sibling(k, j, here, c).wait_send()
        return 0

    def sent_z(k, _):
        for s in range(4):
            to_far(k, s).wait_send()
        for s in range(3):
            to_near(k, s).wait_send()
        for j in range(8):
            z_sibling(k, c, j).wait_send()
        return 0

    lax.fori_loop(0, CHUNKS, sent, 0)
    lax.fori_loop(0, PLANE, sent_plane, 0)
    lax.fori_loop(PLANE, CHUNKS, sent_z, 0)
    for j in range(7):
        slices(j, here).wait_send()
    for g in range(3):
        core_copy(g).wait_send()
        for s in range(4):
            up_copy(s, g).wait_send()
        for s in range(3):
            down_copy(s, g).wait_send()

    for t in range(3):
        level_copy(t).wait_send()

    apart = (y - a // 4 + 4) % 4
    across_x = xl != (a // 2) % 2

    def unpack(strips, block):
        for n in range(4):
            rest = strips[n, STRIP:PACK]
            at = n * STRIP
            block[at : at + STRIP, 0:LANES] = strips[n, 0:STRIP]
            block[at : at + STRIP // 2, LANES:ROWS] = rest[:, 0 : ROWS - LANES]
            block[at + STRIP // 2 : at + STRIP, LANES:ROWS] = rest[:, ROWS - LANES : LANES]

    @pl.when(apart != 1)
    def _():
        pltpu.make_async_copy(rd, rd, f_recv.at[0]).wait()
        unpack(rd, out)

    @pl.when(apart == 1)
    def _():
        out[...] = jnp.zeros_like(out)

    @pl.when(jnp.logical_and(apart != 3, jnp.logical_or(apart != 0, across_x)))
    def _():
        pltpu.make_async_copy(rt, rt, f_recv.at[1]).wait()
        unpack(rt, ft)
        out[...] = out[...] + ft[...].T

    for t in range(3):
        handed_out(t)


def per_device(factors, orbitals, tile_mask):
    dma = pltpu.SemaphoreType.DMA
    vmem = pltpu.VMEM
    part = (SLABS, ROWS, LANES)
    return pl.pallas_call(
        kernel,
        out_shape=jax.ShapeDtypeStruct((ROWS, ROWS), F32),
        in_specs=[
            pl.BlockSpec(memory_space=pl.ANY),
            pl.BlockSpec(memory_space=pltpu.VMEM),
            pl.BlockSpec(memory_space=pltpu.SMEM),
        ],
        out_specs=pl.BlockSpec(memory_space=pltpu.VMEM),
        scratch_shapes=[
            vmem((SLABS, ROWS, 3072), F32),
            vmem((SLABS, ROWS, 3072), BF16),
            vmem((SLABS, ROWS, 3072), BF16),
            vmem((CHUNKS, 2, 8, ROWS, LANES), F32),
            vmem((3072, 2 * LANES), BF16),
            vmem((CHUNKS, *part), F32),
            vmem((2, *part), F32),
            vmem((2, 2, *part), F32),
            vmem((2, 2, *part), F32),
            vmem((2, *part), F32),
            vmem((2, *part), F32),
            vmem((4, PAIR, 3 * SLABS * LANES), BF16),
            vmem((2, PAIR, 3 * SLABS * LANES), BF16),
            vmem((2, 6, 8, PACK, LANES), F32),
            vmem((6, 8, PACK, LANES), F32),
            vmem((4, 6, PACK, LANES), F32),
            vmem((3, 6, PACK, LANES), F32),
            vmem((3, PACK, LANES), F32),
            vmem((3, PACK, LANES), F32),
            vmem((4, PACK, LANES), F32),
            vmem((4, PACK, LANES), F32),
            vmem((ROWS, ROWS), F32),
            dma((SLABS,)),
            dma((CHUNKS, 3)), dma((CHUNKS, 3)),
            dma((CHUNKS, 4, 2)), dma((CHUNKS, 4, 2)),
            dma((CHUNKS, 8)), dma((CHUNKS, 8)),
            dma((7,)), dma((7,)), dma((CHUNKS, 4)), dma((CHUNKS, 4)), dma((CHUNKS, 3)), dma((CHUNKS, 3)),
            dma((CHUNKS, 8)), dma((CHUNKS, 8)),
            dma((CHUNKS, 4)), dma((2,)), dma((2, 2)), dma((2, 2)), dma((2,)), dma((2,)), dma((2,)),
            dma((3,)), dma((3,)),
            dma((4, 3)), dma((4, 3)), dma((3, 3)), dma((3, 3)),
            dma((3,)), dma((3,)),
            dma((3, 2)), dma((2,)),
        ],
        compiler_params=pltpu.CompilerParams(
            collective_id=0, has_side_effects=True, vmem_limit_bytes=60 * 2**20
        ),
    )(factors, orbitals, tile_mask)


def solution(mesh):
    placed = (P("aux", "row", None), P("row", None), P("aux", None, None))
    return jax.shard_map(
        per_device, mesh=mesh, in_specs=placed, out_specs=P("aux", "row"), check_vma=False
    )
```

time: 116 us -> 121 us (1.043)
  the two profiles are of different devices: /device:TPU:39 before, /device:TPU:216 now
where the time goes in v3:
time: 121 us
  Pallas kernels  120 us (99%)
  local copies, waits for them, and re-layouts  1.62 us (1%)
    pallas_call x1, Pallas kernels, per_device(): pl.pallas_call(kernel, out_shape=jax.ShapeDtypeStruct((ROWS, ROWS), F32),...  120 us

profile of v3, /device:TPU:216, one launch (start us, length us, event | category | flops | bytes accessed | tf_op | source)
XLA Modules:
  0.0 121.1 jit_solution(4001322549399583280)
XLA Ops:
  0.0 119.5 %shard_map.37 = f32[192,192]{1,0:T(8,128)} custom-call(f32[3,192,3072]{2,1,0:T(8,128)} %b_hbm.1, f32[192,512]{1,0:T(8,128)} %c_ref.1, s32[3,24,24]{2,1,0:T(8,128)} %mask.1), custom_call_target="tpu_custom_call" | custom-call | tf_op jit(solution)/shard_map/pallas_call | solution.py:537
  119.5 1.6 %copy.5 = f32[192,192]{1,0:T(8,128)} copy(f32[192,192]{1,0:T(8,128)} %shard_map.37) | data formatting | bytes 294912

commit v4 on v3

--- a/solution.py
+++ b/solution.py
@@ -30,7 +30,7 @@
     bf, bh, bl, cb, ch, hs, ho, hy, hx, hw, wr, left, right, kp, rc, rp, rm, re, fp, rd, rt, ft,
     sem_b, y_send, y_recv, x_send, x_recv, s_send, s_recv,
     g_send, g_recv, long_send, long_recv, short_send, short_recv, zs_send, zs_recv,
-    h_send, ho_recv, hy_recv, hx_recv, hw_recv, wr_send, wr_recv,
+    h_send, w_send, ho_recv, hy_recv, hx_recv, hw_recv, wr_send, wr_recv,
     core_send, core_recv, p_send, p_recv, m_send, m_recv, e_send, e_recv, f_send, f_recv,
 ):
     a, r = lax.axis_index("aux"), lax.axis_index("row")
@@ -219,30 +219,45 @@
         return (
             copy(hs.at[k], hy.at[q, c], h_send.at[k, 0], hy_recv.at[q, c], dev(y - 1, xl, h)),
             copy(hs.at[k], hx.at[q, c], h_send.at[k, 1], hx_recv.at[q, c], dev(y, 1 - xl, h)),
-            copy(hs.at[k], wr.at[h], h_send.at[k, 2], wr_recv.at[h], dev(y + 1, xl, c)),
-            copy(hs.at[k], ho.at[q], h_send.at[k, 3], ho_recv.at[q], sibling),
+            copy(hs.at[k], ho.at[q], h_send.at[k, 2], ho_recv.at[q], sibling),
         )
 
+    def w_copy(k, p):
+        h = k % 2
+        return copy(hs.at[k, p], wr.at[h, p], w_send.at[k, p], wr_recv.at[h, p], dev(y + 1, xl, c))
+
+    def w_half(yy, core):
+        return ((yy + 4) % 4 // 2 + core) % 2
+
+    def sends_w(k):
+        return k // 2 == w_half(y + 2, k % 2)
+
     def send_half(k):
-        to_1, to_2, to_3, to_4 = h_copies(k)
+        to_1, to_2, to_3 = h_copies(k)
+
+        @pl.when(sends_w(k))
+        def _():
+            for p in range(SLABS):
+                w_copy(k, p).start()
+
         to_1.start()
         to_2.start()
-        pl.when(k // 2 == 1 - y // 2)(to_3.start)
-        pl.when(k % 2 != c)(to_4.start)
-
-    def relay_copy(k):
+        pl.when(k % 2 != c)(to_3.start)
+
+    def relay_copy(k, p):
         h = k % 2
-        return copy(wr.at[h], hw.at[c], wr_send.at[h], hw_recv.at[c], dev(y + 1, xl, h))
+        return copy(wr.at[h, p], hw.at[c, p], wr_send.at[h, p], hw_recv.at[c, p], dev(y + 1, xl, h))
 
     def relays(k):
-        return k // 2 == 1 - (y + 3) % 4 // 2
-
-    def relay(k):
+        return k // 2 == w_half(y + 1, k % 2)
+
+    def relay(k, slabs=range(SLABS)):
         @pl.when(relays(k))
         def _():
             h = k % 2
-            copy(wr.at[h], wr.at[h], wr_send.at[h], wr_recv.at[h], sibling).wait_recv()
-            relay_copy(k).start()
+            for p in slabs:
+                copy(wr.at[h, p], wr.at[h, p], wr_send.at[h, p], wr_recv.at[h, p], sibling).wait_recv()
+                relay_copy(k, p).start()
 
     plane_slices()
     first(0)
@@ -280,7 +295,6 @@
     whole(3)
     half(3)
     send_half(3)
-    relay(2)
 
     def operand(slot, core, p, value):
         rows = pl.ds(pl.multiple_of(core * ROWS, ROWS), ROWS)
@@ -308,7 +322,7 @@
         lax.fori_loop(0, 2, one, 0)
 
     def kinds_of(g):
-        start, count = ((0, 1), (1, 3), (4, 2))[g]
+        start, count = ((0, 1), (1, 1), (2, 2), (4, 1), (5, 1))[g]
         return pl.ds(start, count)
 
     def core_copy(g):
@@ -320,7 +334,7 @@
         return copy(rc.at[kinds], rc.at[kinds], core_send.at[g], core_recv.at[g], sibling)
 
     def take_o(q):
-        copy(ho.at[q], ho.at[q], h_send.at[2 * q + c, 3], ho_recv.at[q], sibling).wait_recv()
+        copy(ho.at[q], ho.at[q], h_send.at[2 * q + c, 2], ho_recv.at[q], sibling).wait_recv()
         for p in range(SLABS):
             operand(0, c, p, hs[2 * q + c, p])
             operand(0, sib, p, ho[q, p])
@@ -341,15 +355,26 @@
         pl.when(xl == q)(lambda: product(3))
 
     def products_w(q):
-        @pl.when(y // 2 == q)
+        @pl.when(w_half(y, c) == q)
         def _():
-            for core in range(2):
-                copy(hw.at[core], hw.at[core], wr_send.at[core], hw_recv.at[core], sibling).wait_recv()
             for p in range(SLABS):
                 for core in range(2):
+                    piece = hw.at[core, p]
+                    copy(piece, piece, wr_send.at[core, p], hw_recv.at[core, p], sibling).wait_recv()
                     operand(3, core, p, hw[core, p])
             product(4)
+            if q == 1:
+                core_copy(3).start()
             product(5)
+            if q == 1:
+                core_copy(4).start()
+
+        if q == 1:
+
+            @pl.when(w_half(y, c) != q)
+            def _():
+                core_copy(3).start()
+                core_copy(4).start()
 
     mine = jnp.where(xh == y // 2, 0, 1)
 
@@ -388,82 +413,101 @@
         src = rc.at[2 * t + 1 - mine, z]
         return copy(src, re.at[t], e_send.at[t], e_recv.at[t], ((1 - xh) * 8 + z, r))
 
-    def strip_copies(t):
-        i_y = y + (mine, 1 - mine, 2)[t]
-        i_x = (xl + mine) % 2 if t == 1 else xl
-        j_x = xl if t == 1 else (xl + mine) % 2
+    def strip_copies(n):
+        i_y = y + (mine, 1 - mine, 2, 2)[n]
+        i_x = (xl + mine) % 2 if n == 1 else xl
+        j_x = ((xl + mine) % 2, xl, xl, 1 - xl)[n]
         at_i = row_of(i_y, i_x, z // 4)
         at_j = row_of(y, j_x, c)
-        straight = ((at_i, at_j), rd.at[z % 4], f_recv.at[0])
-        turned = ((at_j, at_i), rt.at[z % 4], f_recv.at[1])
-        return straight, turned
-
-    def hand_out(t):
-        level_copy(t).wait_recv()
-        fp[t] = rc[2 * t + mine, z] + re[t]
-        for which, (to, dst, recv) in enumerate(strip_copies(t)):
+        slot = 0 if n < 2 else xh
+        src = fp.at[n] if n < 2 else rc.at[n + 2, z]
+        straight = ((at_i, at_j), rd.at[slot, z % 4], f_recv.at[0])
+        turned = ((at_j, at_i), rt.at[slot, z % 4], f_recv.at[1])
+        return src, straight, turned
+
+    def each_strip(n, local, remote):
+        src, *targets = strip_copies(n)
+        for which, (to, dst, recv) in enumerate(targets):
             own = jnp.logical_and(to[0] == a, to[1] == r)
-            wanted = 2 * t + mine >= which
-
-            @pl.when(jnp.logical_and(wanted, own))
-            def _(dst=dst, recv=recv):
-                pltpu.make_async_copy(fp.at[t], dst, recv).start()
+            wanted = jnp.logical_or(mine == 1, which == 0) if n == 0 else True
+
+            if local is not None:
+
+                @pl.when(jnp.logical_and(wanted, own))
+                def _(dst=dst, recv=recv):
+                    local(pltpu.make_async_copy(src, dst, recv))
 
             @pl.when(jnp.logical_and(wanted, jnp.logical_not(own)))
             def _(dst=dst, recv=recv, to=to, which=which):
-                copy(fp.at[t], dst, f_send.at[t, which], recv, to).start()
-
-    def handed_out(t):
-        for which, (to, dst, recv) in enumerate(strip_copies(t)):
-            own = jnp.logical_and(to[0] == a, to[1] == r)
-
-            @pl.when(jnp.logical_and(2 * t + mine >= which, jnp.logical_not(own)))
-            def _(dst=dst, recv=recv, to=to, which=which):
-                copy(fp.at[t], dst, f_send.at[t, which], recv, to).wait_send()
+                remote(copy(src, dst, f_send.at[n, which], recv, to))
+
+    def hand_out(n):
+        if n < 2:
+            level_copy(n).wait_recv()
+            fp[n] = rc[2 * n + mine, z] + re[n]
+        each_strip(n, lambda one: one.start(), lambda one: one.start())
+
+    def handed_out(n):
+        each_strip(n, None, lambda one: one.wait_send())
 
     take_o(0)
     product(0)
     take_y_x(0)
     products_y_x(0)
+    relay(2)
     products_w(0)
-    relay(3)
+    relay(3, (0,))
     take_o(1)
     product(0)
     core_copy(0).start()
+    relay(3, (1, 2))
     take_y_x(1)
-    products_y_x(1)
+    product(1)
     core_copy(1).start()
+    product(2)
+    pl.when(xl == 1)(lambda: product(3))
+    core_copy(2).start()
     sum_step(0, 0)
     sum_step(0, 1)
     sum_step(1, 0)
+    sum_step(0, 2)
+    products_w(1)
     sum_step(1, 1)
-    products_w(1)
-    core_copy(2).start()
     sum_step(2, 0)
+    sum_step(1, 2)
+    sum_step(0, 3)
     sum_step(2, 1)
-    sum_step(0, 2)
+    sum_step(0, 4)
     sum_step(3, 0)
+    sum_step(2, 2)
+    sum_step(1, 3)
     sum_step(3, 1)
-    sum_step(1, 2)
+    sum_step(1, 4)
     sum_step(4, 0)
+    sum_step(3, 2)
+    sum_step(2, 3)
     sum_step(4, 1)
     level_copy(0).start()
+    sum_step(2, 4)
+    sum_step(4, 2)
     level_copy(1).start()
-    sum_step(2, 2)
+    sum_step(3, 3)
+    sum_step(3, 4)
     hand_out(0)
+    sum_step(4, 3)
+    hand_out(2)
+    sum_step(4, 4)
+    hand_out(3)
     hand_out(1)
-    sum_step(3, 2)
-    sum_step(4, 2)
-    level_copy(2).start()
-    hand_out(2)
 
     def sent(k, _):
-        to_1, to_2, to_3, to_4 = h_copies(k)
+        to_1, to_2, to_3 = h_copies(k)
         to_1.wait_send()
         to_2.wait_send()
-        pl.when(k // 2 == 1 - y // 2)(to_3.wait_send)
-        pl.when(k % 2 != c)(to_4.wait_send)
-        pl.when(relays(k))(relay_copy(k).wait_send)
+        pl.when(k % 2 != c)(to_3.wait_send)
+        for p in range(SLABS):
+            pl.when(sends_w(k))(w_copy(k, p).wait_send)
+            pl.when(relays(k))(relay_copy(k, p).wait_send)
         return 0
 
     def sent_plane(k, _):
@@ -490,31 +534,39 @@
     lax.fori_loop(PLANE, CHUNKS, sent_z, 0)
     for j in range(7):
         slices(j, here).wait_send()
-    for g in range(3):
+    for g in range(5):
         core_copy(g).wait_send()
         for s in range(4):
             up_copy(s, g).wait_send()
         for s in range(3):
             down_copy(s, g).wait_send()
 
-    for t in range(3):
+    for t in range(2):
         level_copy(t).wait_send()
 
     apart = (y - a // 4 + 4) % 4
     across_x = xl != (a // 2) % 2
 
-    def unpack(strips, block):
+    def gather(strips, sem, block):
+        @pl.when(apart == 2)
+        def _():
+            pltpu.make_async_copy(strips, strips, sem).wait()
+            strips[0] = strips[0] + strips[1]
+
+        @pl.when(apart != 2)
+        def _():
+            pltpu.make_async_copy(strips.at[0], strips.at[0], sem).wait()
+
         for n in range(4):
-            rest = strips[n, STRIP:PACK]
+            rest = strips[0, n, STRIP:PACK]
             at = n * STRIP
-            block[at : at + STRIP, 0:LANES] = strips[n, 0:STRIP]
+            block[at : at + STRIP, 0:LANES] = strips[0, n, 0:STRIP]
             block[at : at + STRIP // 2, LANES:ROWS] = rest[:, 0 : ROWS - LANES]
             block[at + STRIP // 2 : at + STRIP, LANES:ROWS] = rest[:, ROWS - LANES : LANES]
 
     @pl.when(apart != 1)
     def _():
-        pltpu.make_async_copy(rd, rd, f_recv.at[0]).wait()
-        unpack(rd, out)
+        gather(rd, f_recv.at[0], out)
 
     @pl.when(apart == 1)
     def _():
@@ -522,12 +574,11 @@
 
     @pl.when(jnp.logical_and(apart != 3, jnp.logical_or(apart != 0, across_x)))
     def _():
-        pltpu.make_async_copy(rt, rt, f_recv.at[1]).wait()
-        unpack(rt, ft)
+        gather(rt, f_recv.at[1], ft)
         out[...] = out[...] + ft[...].T
 
-    for t in range(3):
-        handed_out(t)
+    for n in range(4):
+        handed_out(n)
 
 
 def per_device(factors, orbitals, tile_mask):
@@ -561,10 +612,10 @@
             vmem((6, 8, PACK, LANES), F32),
             vmem((4, 6, PACK, LANES), F32),
             vmem((3, 6, PACK, LANES), F32),
-            vmem((3, PACK, LANES), F32),
-            vmem((3, PACK, LANES), F32),
-            vmem((4, PACK, LANES), F32),
-            vmem((4, PACK, LANES), F32),
+            vmem((2, PACK, LANES), F32),
+            vmem((2, PACK, LANES), F32),
+            vmem((2, 4, PACK, LANES), F32),
+            vmem((2, 4, PACK, LANES), F32),
             vmem((ROWS, ROWS), F32),
             dma((SLABS,)),
             dma((CHUNKS, 3)), dma((CHUNKS, 3)),
@@ -572,11 +623,12 @@
             dma((CHUNKS, 8)), dma((CHUNKS, 8)),
             dma((7,)), dma((7,)), dma((CHUNKS, 4)), dma((CHUNKS, 4)), dma((CHUNKS, 3)), dma((CHUNKS, 3)),
             dma((CHUNKS, 8)), dma((CHUNKS, 8)),
-            dma((CHUNKS, 4)), dma((2,)), dma((2, 2)), dma((2, 2)), dma((2,)), dma((2,)), dma((2,)),
-            dma((3,)), dma((3,)),
-            dma((4, 3)), dma((4, 3)), dma((3, 3)), dma((3, 3)),
-            dma((3,)), dma((3,)),
-            dma((3, 2)), dma((2,)),
+            dma((CHUNKS, 3)), dma((CHUNKS, SLABS)), dma((2,)), dma((2, 2)), dma((2, 2)),
+            dma((2, SLABS)), dma((2, SLABS)), dma((2, SLABS)),
+            dma((5,)), dma((5,)),
+            dma((4, 5)), dma((4, 5)), dma((3, 5)), dma((3, 5)),
+            dma((2,)), dma((2,)),
+            dma((4, 2)), dma((2,)),
         ],
         compiler_params=pltpu.CompilerParams(
             collective_id=0, has_side_effects=True, vmem_limit_bytes=60 * 2**20

time: 121 us -> 107 us (0.88)
  the two profiles are of different devices: /device:TPU:216 before, /device:TPU:44 now
where the time goes in v4:
time: 107 us
  Pallas kernels  105 us (98%)
  local copies, waits for them, and re-layouts  1.62 us (2%)
    pallas_call x1, Pallas kernels, per_device(): pl.pallas_call(kernel, out_shape=jax.ShapeDtypeStruct((ROWS, ROWS), F32),...  105 us

profile of v4, /device:TPU:44, one launch (start us, length us, event | category | flops | bytes accessed | tf_op | source)
XLA Modules:
  0.0 107.1 jit_solution(5193457768615706909)
XLA Ops:
  0.0 105.5 %shard_map.37 = f32[192,192]{1,0:T(8,128)} custom-call(f32[3,192,3072]{2,1,0:T(8,128)} %b_hbm.1, f32[192,512]{1,0:T(8,128)} %c_ref.1, s32[3,24,24]{2,1,0:T(8,128)} %mask.1), custom_call_target="tpu_custom_call" | custom-call | tf_op jit(solution)/shard_map/pallas_call | solution.py:588
  105.5 1.6 %copy.5 = f32[192,192]{1,0:T(8,128)} copy(f32[192,192]{1,0:T(8,128)} %shard_map.37) | data formatting | bytes 294912

commit v5 on v4

--- a/solution.py
+++ b/solution.py
@@ -206,20 +206,19 @@
 
         lax.fori_loop(0, 16, block, 0)
 
-        def slab(p, _):
+        for p in range(SLABS):
             both = jnp.dot(bh[p], ch[...], preferred_element_type=F32)
             low = jnp.dot(bl[p], ch[:, 0:LANES], preferred_element_type=F32)
             hs[k, p] = both[:, 0:LANES] + (both[:, LANES : 2 * LANES] + low)
-            return 0
-
-        lax.fori_loop(0, SLABS, slab, 0)
-
-    def h_copies(k):
+            send_half(k, p)
+
+    def h_copies(k, p=slice(None)):
         h, q = k % 2, k // 2
+        src = hs.at[k, p]
         return (
-            copy(hs.at[k], hy.at[q, c], h_send.at[k, 0], hy_recv.at[q, c], dev(y - 1, xl, h)),
-            copy(hs.at[k], hx.at[q, c], h_send.at[k, 1], hx_recv.at[q, c], dev(y, 1 - xl, h)),
-            copy(hs.at[k], ho.at[q], h_send.at[k, 2], ho_recv.at[q], sibling),
+            copy(src, hy.at[q, c, p], h_send.at[k, 0], hy_recv.at[q, c], dev(y - 1, xl, h)),
+            copy(src, hx.at[q, c, p], h_send.at[k, 1], hx_recv.at[q, c], dev(y, 1 - xl, h)),
+            copy(src, ho.at[q, p], h_send.at[k, 2], ho_recv.at[q], sibling),
         )
 
     def w_copy(k, p):
@@ -232,14 +231,9 @@
     def sends_w(k):
         return k // 2 == w_half(y + 2, k % 2)
 
-    def send_half(k):
-        to_1, to_2, to_3 = h_copies(k)
-
-        @pl.when(sends_w(k))
-        def _():
-            for p in range(SLABS):
-                w_copy(k, p).start()
-
+    def send_half(k, p):
+        pl.when(sends_w(k))(w_copy(k, p).start)
+        to_1, to_2, to_3 = h_copies(k, p)
         to_1.start()
         to_2.start()
         pl.when(k % 2 != c)(to_3.start)
@@ -265,36 +259,32 @@
     screen(0)
     z_first()
     z_own(2)
+    z_own(3)
     forward_y(0)
     first(1)
     screen(1)
     z_step(2, 0)
+    z_step(3, 0)
     forward_x(0)
     forward_y(1)
-    z_own(3)
     screen(2)
     z_step(2, 1)
     whole(0)
     half(0)
-    send_half(0)
     forward_x(1)
+    z_step(3, 1)
     z_step(2, 2)
-    z_step(3, 0)
     whole(1)
     half(1)
-    send_half(1)
+    z_step(3, 2)
     z_step(2, 3)
-    z_step(3, 1)
     whole(2)
     half(2)
-    send_half(2)
-    z_step(3, 2)
     z_step(3, 3)
     relay(0)
     relay(1)
     whole(3)
     half(3)
-    send_half(3)
 
     def operand(slot, core, p, value):
         rows = pl.ds(pl.multiple_of(core * ROWS, ROWS), ROWS)
@@ -378,13 +368,19 @@
 
     mine = jnp.where(xh == y // 2, 0, 1)
 
-    def up_copy(s, g):
-        src = rc.at[kinds_of(g), (z + 4 - s) % 8]
-        return copy(src, rp.at[s, kinds_of(g)], p_send.at[s, g], p_recv.at[s, g], z_up)
-
-    def down_copy(s, g):
-        src = rc.at[kinds_of(g), (z + 5 + s) % 8]
-        return copy(src, rm.at[s, kinds_of(g)], m_send.at[s, g], m_recv.at[s, g], z_down)
+    def far_slice(s):
+        return (z + 8 + far * (4 - s)) % 8
+
+    def near_slice(s):
+        return (z + 8 - far * (3 - s)) % 8
+
+    def far_copy(s, g):
+        src = rc.at[kinds_of(g), far_slice(s)]
+        return copy(src, rp.at[s, kinds_of(g)], p_send.at[s, g], p_recv.at[s, g], z_far)
+
+    def near_copy(s, g):
+        src = rc.at[kinds_of(g), near_slice(s)]
+        return copy(src, rm.at[s, kinds_of(g)], m_send.at[s, g], m_recv.at[s, g], z_near)
 
     def sum_step(s, g):
         kinds = kinds_of(g)
@@ -397,33 +393,31 @@
 
             lax.fori_loop(0, 8, add, 0)
         else:
-            up_copy(s - 1, g).wait_recv()
-            d = (z + 4 - s) % 8
+            far_copy(s - 1, g).wait_recv()
+            d = far_slice(s)
             rc[kinds, d] = rc[kinds, d] + rp[s - 1, kinds]
             if s < 4:
-                down_copy(s - 1, g).wait_recv()
-                d = (z + 5 + s) % 8
+                near_copy(s - 1, g).wait_recv()
+                d = near_slice(s)
                 rc[kinds, d] = rc[kinds, d] + rm[s - 1, kinds]
         if s < 4:
-            up_copy(s, g).start()
+            far_copy(s, g).start()
         if s < 3:
-            down_copy(s, g).start()
+            near_copy(s, g).start()
 
     def level_copy(t):
         src = rc.at[2 * t + 1 - mine, z]
         return copy(src, re.at[t], e_send.at[t], e_recv.at[t], ((1 - xh) * 8 + z, r))
 
     def strip_copies(n):
-        i_y = y + (mine, 1 - mine, 2, 2)[n]
+        i_y = y + (mine, 1 - mine, 2)[n]
         i_x = (xl + mine) % 2 if n == 1 else xl
-        j_x = ((xl + mine) % 2, xl, xl, 1 - xl)[n]
+        j_x = xl if n == 1 else (xl + mine) % 2
         at_i = row_of(i_y, i_x, z // 4)
         at_j = row_of(y, j_x, c)
-        slot = 0 if n < 2 else xh
-        src = fp.at[n] if n < 2 else rc.at[n + 2, z]
-        straight = ((at_i, at_j), rd.at[slot, z % 4], f_recv.at[0])
-        turned = ((at_j, at_i), rt.at[slot, z % 4], f_recv.at[1])
-        return src, straight, turned
+        straight = ((at_i, at_j), rd.at[z % 4], f_recv.at[0])
+        turned = ((at_j, at_i), rt.at[z % 4], f_recv.at[1])
+        return fp.at[n], straight, turned
 
     def each_strip(n, local, remote):
         src, *targets = strip_copies(n)
@@ -442,9 +436,8 @@
                 remote(copy(src, dst, f_send.at[n, which], recv, to))
 
     def hand_out(n):
-        if n < 2:
-            level_copy(n).wait_recv()
-            fp[n] = rc[2 * n + mine, z] + re[n]
+        level_copy(n).wait_recv()
+        fp[n] = rc[2 * n + mine, z] + re[n]
         each_strip(n, lambda one: one.start(), lambda one: one.start())
 
     def handed_out(n):
@@ -453,14 +446,14 @@
     take_o(0)
     product(0)
     take_y_x(0)
+    relay(2)
     products_y_x(0)
-    relay(2)
+    relay(3, (0,))
     products_w(0)
-    relay(3, (0,))
+    relay(3, (1, 2))
     take_o(1)
     product(0)
     core_copy(0).start()
-    relay(3, (1, 2))
     take_y_x(1)
     product(1)
     core_copy(1).start()
@@ -473,32 +466,32 @@
     sum_step(0, 2)
     products_w(1)
     sum_step(1, 1)
+    sum_step(0, 3)
+    sum_step(0, 4)
     sum_step(2, 0)
     sum_step(1, 2)
-    sum_step(0, 3)
     sum_step(2, 1)
-    sum_step(0, 4)
+    sum_step(1, 3)
+    sum_step(1, 4)
     sum_step(3, 0)
     sum_step(2, 2)
-    sum_step(1, 3)
     sum_step(3, 1)
-    sum_step(1, 4)
+    sum_step(2, 3)
+    sum_step(2, 4)
     sum_step(4, 0)
     sum_step(3, 2)
-    sum_step(2, 3)
     sum_step(4, 1)
     level_copy(0).start()
-    sum_step(2, 4)
+    sum_step(3, 3)
+    sum_step(3, 4)
     sum_step(4, 2)
     level_copy(1).start()
-    sum_step(3, 3)
-    sum_step(3, 4)
+    sum_step(4, 3)
+    sum_step(4, 4)
+    level_copy(2).start()
     hand_out(0)
-    sum_step(4, 3)
+    hand_out(1)
     hand_out(2)
-    sum_step(4, 4)
-    hand_out(3)
-    hand_out(1)
 
     def sent(k, _):
         to_1, to_2, to_3 = h_copies(k)
@@ -537,30 +530,22 @@
     for g in range(5):
         core_copy(g).wait_send()
         for s in range(4):
-            up_copy(s, g).wait_send()
+            far_copy(s, g).wait_send()
         for s in range(3):
-            down_copy(s, g).wait_send()
-
-    for t in range(2):
+            near_copy(s, g).wait_send()
+
+    for t in range(3):
         level_copy(t).wait_send()
 
     apart = (y - a // 4 + 4) % 4
     across_x = xl != (a // 2) % 2
 
     def gather(strips, sem, block):
-        @pl.when(apart == 2)
-        def _():
-            pltpu.make_async_copy(strips, strips, sem).wait()
-            strips[0] = strips[0] + strips[1]
-
-        @pl.when(apart != 2)
-        def _():
-            pltpu.make_async_copy(strips.at[0], strips.at[0], sem).wait()
-
+        pltpu.make_async_copy(strips, strips, sem).wait()
         for n in range(4):
-            rest = strips[0, n, STRIP:PACK]
+            rest = strips[n, STRIP:PACK]
             at = n * STRIP
-            block[at : at + STRIP, 0:LANES] = strips[0, n, 0:STRIP]
+            block[at : at + STRIP, 0:LANES] = strips[n, 0:STRIP]
             block[at : at + STRIP // 2, LANES:ROWS] = rest[:, 0 : ROWS - LANES]
             block[at + STRIP // 2 : at + STRIP, LANES:ROWS] = rest[:, ROWS - LANES : LANES]
 
@@ -577,7 +562,7 @@
         gather(rt, f_recv.at[1], ft)
         out[...] = out[...] + ft[...].T
 
-    for n in range(4):
+    for n in range(3):
         handed_out(n)
 
 
@@ -612,10 +597,10 @@
             vmem((6, 8, PACK, LANES), F32),
             vmem((4, 6, PACK, LANES), F32),
             vmem((3, 6, PACK, LANES), F32),
-            vmem((2, PACK, LANES), F32),
-            vmem((2, PACK, LANES), F32),
-            vmem((2, 4, PACK, LANES), F32),
-            vmem((2, 4, PACK, LANES), F32),
+            vmem((3, PACK, LANES), F32),
+            vmem((3, PACK, LANES), F32),
+            vmem((4, PACK, LANES), F32),
+            vmem((4, PACK, LANES), F32),
             vmem((ROWS, ROWS), F32),
             dma((SLABS,)),
             dma((CHUNKS, 3)), dma((CHUNKS, 3)),
@@ -627,8 +612,8 @@
             dma((2, SLABS)), dma((2, SLABS)), dma((2, SLABS)),
             dma((5,)), dma((5,)),
             dma((4, 5)), dma((4, 5)), dma((3, 5)), dma((3, 5)),
-            dma((2,)), dma((2,)),
-            dma((4, 2)), dma((2,)),
+            dma((3,)), dma((3,)),
+            dma((3, 2)), dma((2,)),
         ],
         compiler_params=pltpu.CompilerParams(
             collective_id=0, has_side_effects=True, vmem_limit_bytes=60 * 2**20

time: 107 us -> 105 us (0.981)
  the two profiles are of different devices: /device:TPU:44 before, /device:TPU:4 now
where the time goes in v5:
time: 105 us
  Pallas kernels  104 us (99%)
  local copies, waits for them, and re-layouts  1.62 us (2%)
    pallas_call x1, Pallas kernels, per_device(): pl.pallas_call(kernel, out_shape=jax.ShapeDtypeStruct((ROWS, ROWS), F32),...  104 us

profile of v5, /device:TPU:4, one launch (start us, length us, event | category | flops | bytes accessed | tf_op | source)
XLA Modules:
  0.0 105.2 jit_solution(14732122752003127461)
XLA Ops:
  0.0 103.5 %shard_map.37 = f32[192,192]{1,0:T(8,128)} custom-call(f32[3,192,3072]{2,1,0:T(8,128)} %b_hbm.1, f32[192,512]{1,0:T(8,128)} %c_ref.1, s32[3,24,24]{2,1,0:T(8,128)} %mask.1), custom_call_target="tpu_custom_call" | custom-call | tf_op jit(solution)/shard_map/pallas_call | solution.py:573
  103.5 1.6 %copy.5 = f32[192,192]{1,0:T(8,128)} copy(f32[192,192]{1,0:T(8,128)} %shard_map.37) | data formatting | bytes 294912

commit v6 on v5

--- a/solution.py
+++ b/solution.py
@@ -1,3 +1,5 @@
+import functools
+
 import jax
 import jax.numpy as jnp
 from jax import lax
@@ -27,11 +29,11 @@
 
 def kernel(
     b_hbm, c_ref, mask, out,
-    bf, bh, bl, cb, ch, hs, ho, hy, hx, hw, wr, left, right, kp, rc, rp, rm, re, fp, rd, rt, ft,
+    bf, bh, bl, cb, ch, hs, ho, hy, hx, hw, wr, left, right, kp, rc, rp, rm, fin, fp, rd, rt, ft,
     sem_b, y_send, y_recv, x_send, x_recv, s_send, s_recv,
     g_send, g_recv, long_send, long_recv, short_send, short_recv, zs_send, zs_recv,
     h_send, w_send, ho_recv, hy_recv, hx_recv, hw_recv, wr_send, wr_recv,
-    core_send, core_recv, p_send, p_recv, m_send, m_recv, e_send, e_recv, f_send, f_recv,
+    core_send, core_recv, p_send, p_recv, m_send, m_recv, l_send, l_recv, f_send, f_recv,
 ):
     a, r = lax.axis_index("aux"), lax.axis_index("row")
     xh, z = a // 8, a % 8
@@ -295,21 +297,16 @@
             for where, part in ((0, high), (1, high), (2, low)):
                 right[slot // 2, rows, pl.ds((where * SLABS + p) * LANES, LANES)] = part
 
-    def product(kind):
+    def product(kind, core):
         rows, columns = ((0, 0), (1, 1), (1, 0), (2, 0), (3, 0), (3, 1))[kind]
-
-        def one(core, _):
-            at = pl.ds(pl.multiple_of(core * ROWS, ROWS), ROWS)
-            value = lax.dot_general(
-                left[rows], right[columns, at], (((1,), (1,)), ((), ())), preferred_element_type=F32
-            )
-            rest = value[:, LANES:ROWS].reshape(8, 2, STRIP // 2, ROWS - LANES)
-            rest = jnp.concatenate([rest[:, 0], rest[:, 1]], axis=-1)
-            kp[core, kind, :, 0:STRIP] += value[:, 0:LANES].reshape(8, STRIP, LANES)
-            kp[core, kind, :, STRIP:PACK] += rest
-            return 0
-
-        lax.fori_loop(0, 2, one, 0)
+        at = pl.ds(pl.multiple_of(core * ROWS, ROWS), ROWS)
+        value = lax.dot_general(
+            left[rows], right[columns, at], (((1,), (1,)), ((), ())), preferred_element_type=F32
+        )
+        rest = value[:, LANES:ROWS].reshape(8, 2, STRIP // 2, ROWS - LANES)
+        rest = jnp.concatenate([rest[:, 0], rest[:, 1]], axis=-1)
+        kp[core, kind, :, 0:STRIP] += value[:, 0:LANES].reshape(8, STRIP, LANES)
+        kp[core, kind, :, STRIP:PACK] += rest
 
     def kinds_of(g):
         start, count = ((0, 1), (1, 1), (2, 2), (4, 1), (5, 1))[g]
@@ -340,9 +337,14 @@
                 operand(2, core, p, hx[q, core, p])
 
     def products_y_x(q):
-        product(1)
-        product(2)
-        pl.when(xl == q)(lambda: product(3))
+        for core in (sib, c):
+            product(1, core)
+            if q == 1 and core is sib:
+                core_copy(1).start()
+            product(2, core)
+            pl.when(xl == q)(functools.partial(product, 3, core))
+            if q == 1 and core is sib:
+                core_copy(2).start()
 
     def products_w(q):
         @pl.when(w_half(y, c) == q)
@@ -352,12 +354,14 @@
                     piece = hw.at[core, p]
                     copy(piece, piece, wr_send.at[core, p], hw_recv.at[core, p], sibling).wait_recv()
                     operand(3, core, p, hw[core, p])
-            product(4)
+            product(4, sib)
             if q == 1:
                 core_copy(3).start()
-            product(5)
+            product(5, sib)
             if q == 1:
                 core_copy(4).start()
+            product(4, c)
+            product(5, c)
 
         if q == 1:
 
@@ -382,8 +386,16 @@
         src = rc.at[kinds_of(g), near_slice(s)]
         return copy(src, rm.at[s, kinds_of(g)], m_send.at[s, g], m_recv.at[s, g], z_near)
 
+    def last_copy(which, kind):
+        same = mine == kind % 2
+        at = 4 if which == 2 else jnp.where(same, which, which + 2)
+        piece = (z, far_slice(3), near_slice(2))[(which + 1) % 3]
+        to = jnp.where(same, xh, 1 - xh) * 8 + piece
+        return copy(rc.at[kind, piece], fin.at[at, kind], l_send.at[which, kind], l_recv.at[at, kind], (to, r))
+
     def sum_step(s, g):
         kinds = kinds_of(g)
+        each_kind = range(kinds.start, kinds.start + kinds.size)
         if s == 0:
             core_arrival(g).wait_recv()
 
@@ -396,18 +408,23 @@
             far_copy(s - 1, g).wait_recv()
             d = far_slice(s)
             rc[kinds, d] = rc[kinds, d] + rp[s - 1, kinds]
-            if s < 4:
+            if s < 3:
                 near_copy(s - 1, g).wait_recv()
                 d = near_slice(s)
                 rc[kinds, d] = rc[kinds, d] + rm[s - 1, kinds]
-        if s < 4:
+        if s < 3:
             far_copy(s, g).start()
-        if s < 3:
+        else:
+            for kind in each_kind:
+                last_copy(0, kind).start()
+        if s < 2:
             near_copy(s, g).start()
-
-    def level_copy(t):
-        src = rc.at[2 * t + 1 - mine, z]
-        return copy(src, re.at[t], e_send.at[t], e_recv.at[t], ((1 - xh) * 8 + z, r))
+        elif s == 2:
+            for kind in each_kind:
+                last_copy(1, kind).start()
+        if s == 0:
+            for kind in each_kind:
+                pl.when(mine != kind % 2)(last_copy(2, kind).start)
 
     def strip_copies(n):
         i_y = y + (mine, 1 - mine, 2)[n]
@@ -436,15 +453,19 @@
                 remote(copy(src, dst, f_send.at[n, which], recv, to))
 
     def hand_out(n):
-        level_copy(n).wait_recv()
-        fp[n] = rc[2 * n + mine, z] + re[n]
+        kind = 2 * n + mine
+        for at in range(5):
+            piece = fin.at[at, kind]
+            copy(piece, piece, l_send.at[0, kind], l_recv.at[at, kind], sibling).wait_recv()
+        fp[n] = (rc[kind, z] + fin[0, kind] + fin[1, kind]) + (fin[2, kind] + fin[3, kind] + fin[4, kind])
         each_strip(n, lambda one: one.start(), lambda one: one.start())
 
     def handed_out(n):
         each_strip(n, None, lambda one: one.wait_send())
 
     take_o(0)
-    product(0)
+    product(0, sib)
+    product(0, c)
     take_y_x(0)
     relay(2)
     products_y_x(0)
@@ -452,14 +473,11 @@
     products_w(0)
     relay(3, (1, 2))
     take_o(1)
-    product(0)
+    product(0, sib)
     core_copy(0).start()
+    product(0, c)
     take_y_x(1)
-    product(1)
-    core_copy(1).start()
-    product(2)
-    pl.when(xl == 1)(lambda: product(3))
-    core_copy(2).start()
+    products_y_x(1)
     sum_step(0, 0)
     sum_step(0, 1)
     sum_step(1, 0)
@@ -478,17 +496,9 @@
     sum_step(3, 1)
     sum_step(2, 3)
     sum_step(2, 4)
-    sum_step(4, 0)
     sum_step(3, 2)
-    sum_step(4, 1)
-    level_copy(0).start()
     sum_step(3, 3)
     sum_step(3, 4)
-    sum_step(4, 2)
-    level_copy(1).start()
-    sum_step(4, 3)
-    sum_step(4, 4)
-    level_copy(2).start()
     hand_out(0)
     hand_out(1)
     hand_out(2)
@@ -529,13 +539,15 @@
         slices(j, here).wait_send()
     for g in range(5):
         core_copy(g).wait_send()
-        for s in range(4):
+        for s in range(3):
             far_copy(s, g).wait_send()
-        for s in range(3):
+        for s in range(2):
             near_copy(s, g).wait_send()
 
-    for t in range(3):
-        level_copy(t).wait_send()
+    for kind in range(6):
+        for which in range(2):
+            last_copy(which, kind).wait_send()
+        pl.when(mine != kind % 2)(last_copy(2, kind).wait_send)
 
     apart = (y - a // 4 + 4) % 4
     across_x = xl != (a // 2) % 2
@@ -595,9 +607,9 @@
             vmem((2, PAIR, 3 * SLABS * LANES), BF16),
             vmem((2, 6, 8, PACK, LANES), F32),
             vmem((6, 8, PACK, LANES), F32),
-            vmem((4, 6, PACK, LANES), F32),
             vmem((3, 6, PACK, LANES), F32),
-            vmem((3, PACK, LANES), F32),
+            vmem((2, 6, PACK, LANES), F32),
+            vmem((5, 6, PACK, LANES), F32),
             vmem((3, PACK, LANES), F32),
             vmem((4, PACK, LANES), F32),
             vmem((4, PACK, LANES), F32),
@@ -611,8 +623,8 @@
             dma((CHUNKS, 3)), dma((CHUNKS, SLABS)), dma((2,)), dma((2, 2)), dma((2, 2)),
             dma((2, SLABS)), dma((2, SLABS)), dma((2, SLABS)),
             dma((5,)), dma((5,)),
-            dma((4, 5)), dma((4, 5)), dma((3, 5)), dma((3, 5)),
-            dma((3,)), dma((3,)),
+            dma((3, 5)), dma((3, 5)), dma((2, 5)), dma((2, 5)),
+            dma((3, 6)), dma((5, 6)),
             dma((3, 2)), dma((2,)),
         ],
         compiler_params=pltpu.CompilerParams(

time: 105 us -> 99.1 us (0.944)
  the two profiles are of different devices: /device:TPU:4 before, /device:TPU:2 now
where the time goes in v6:
time: 99.1 us; the launch traced here: 99 us
  Pallas kernels  97.3 us (98%)
  local copies, waits for them, and re-layouts  1.62 us (2%)
    pallas_call x1, Pallas kernels, per_device(): pl.pallas_call(kernel, out_shape=jax.ShapeDtypeStruct((ROWS, ROWS), F32),...  97.3 us

profile of v6, /device:TPU:2, one launch (start us, length us, event | category | flops | bytes accessed | tf_op | source)
XLA Modules:
  0.0 99.0 jit_solution(15226835641285257043)
XLA Ops:
  0.0 97.3 %shard_map.37 = f32[192,192]{1,0:T(8,128)} custom-call(f32[3,192,3072]{2,1,0:T(8,128)} %b_hbm.1, f32[192,512]{1,0:T(8,128)} %c_ref.1, s32[3,24,24]{2,1,0:T(8,128)} %mask.1), custom_call_target="tpu_custom_call" | custom-call | tf_op jit(solution)/shard_map/pallas_call | solution.py:585
  97.3 1.6 %copy.5 = f32[192,192]{1,0:T(8,128)} copy(f32[192,192]{1,0:T(8,128)} %shard_map.37) | data formatting | bytes 294912

commit v7 on v6

--- a/solution.py
+++ b/solution.py
@@ -305,8 +305,12 @@
         )
         rest = value[:, LANES:ROWS].reshape(8, 2, STRIP // 2, ROWS - LANES)
         rest = jnp.concatenate([rest[:, 0], rest[:, 1]], axis=-1)
-        kp[core, kind, :, 0:STRIP] += value[:, 0:LANES].reshape(8, STRIP, LANES)
-        kp[core, kind, :, STRIP:PACK] += rest
+        body = value[:, 0:LANES].reshape(8, STRIP, LANES)
+        base = 4 * ((y + (0, 1, 0, 2)[rows]) % 2) + 2 * ((xl + (rows == 2)) % 2)
+        for n in range(8):
+            at_z = (base + 8 + (-n if n < 4 else n - 3)) % 8
+            kp[core, kind, at_z, 0:STRIP] += body[n]
+            kp[core, kind, at_z, STRIP:PACK] += rest[n]
 
     def kinds_of(g):
         start, count = ((0, 1), (1, 1), (2, 2), (4, 1), (5, 1))[g]
@@ -430,10 +434,13 @@
         i_y = y + (mine, 1 - mine, 2)[n]
         i_x = (xl + mine) % 2 if n == 1 else xl
         j_x = xl if n == 1 else (xl + mine) % 2
-        at_i = row_of(i_y, i_x, z // 4)
+        above = (z + 8 - (4 * (i_y % 2) + 2 * i_x)) % 8
+        upper = jnp.logical_and(above >= 1, above <= 4)
+        strip = jnp.where(upper, above - 1, (8 - above) % 8)
+        at_i = row_of(i_y, i_x, jnp.where(upper, 1, 0))
         at_j = row_of(y, j_x, c)
-        straight = ((at_i, at_j), rd.at[z % 4], f_recv.at[0])
-        turned = ((at_j, at_i), rt.at[z % 4], f_recv.at[1])
+        straight = ((at_i, at_j), rd.at[strip], f_recv.at[0])
+        turned = ((at_j, at_i), rt.at[strip], f_recv.at[1])
         return fp.at[n], straight, turned
 
     def each_strip(n, local, remote):
@@ -480,26 +487,26 @@
     products_y_x(1)
     sum_step(0, 0)
     sum_step(0, 1)
+    sum_step(0, 2)
     sum_step(1, 0)
-    sum_step(0, 2)
     products_w(1)
     sum_step(1, 1)
     sum_step(0, 3)
     sum_step(0, 4)
+    sum_step(1, 2)
     sum_step(2, 0)
-    sum_step(1, 2)
     sum_step(2, 1)
     sum_step(1, 3)
     sum_step(1, 4)
     sum_step(3, 0)
+    sum_step(3, 1)
     sum_step(2, 2)
-    sum_step(3, 1)
     sum_step(2, 3)
     sum_step(2, 4)
     sum_step(3, 2)
+    hand_out(0)
     sum_step(3, 3)
     sum_step(3, 4)
-    hand_out(0)
     hand_out(1)
     hand_out(2)
 

time: 99.1 us -> 99.1 us (level)
  no operation moved by 1% of the time
where the time goes in v7:
time: 99.1 us; the launch traced here: 99 us
  Pallas kernels  97.3 us (98%)
  local copies, waits for them, and re-layouts  1.62 us (2%)
    pallas_call x1, Pallas kernels, per_device(): pl.pallas_call(kernel, out_shape=jax.ShapeDtypeStruct((ROWS, ROWS), F32),...  97.3 us

profile of v7, /device:TPU:2, one launch (start us, length us, event | category | flops | bytes accessed | tf_op | source)
XLA Modules:
  0.0 99.0 jit_solution(1129457927203814132)
XLA Ops:
  0.0 97.3 %shard_map.37 = f32[192,192]{1,0:T(8,128)} custom-call(f32[3,192,3072]{2,1,0:T(8,128)} %b_hbm.1, f32[192,512]{1,0:T(8,128)} %c_ref.1, s32[3,24,24]{2,1,0:T(8,128)} %mask.1), custom_call_target="tpu_custom_call" | custom-call | tf_op jit(solution)/shard_map/pallas_call | solution.py:592
  97.3 1.6 %copy.5 = f32[192,192]{1,0:T(8,128)} copy(f32[192,192]{1,0:T(8,128)} %shard_map.37) | data formatting | bytes 294912
